TPU v7x, 32 devices: a whole 2x2x4 slice. The times are simulated.
32 devices in a mesh: rep: 4 (over y, core), fsdp: 8 (over z, x).
Axes of the slice: x: 2, y: 2, z: 4, core: 2. Of those that a mesh axis runs over, the one named last changes fastest.
Arguments:
- clip_tokens: bfloat16 [4096, 6144], P(('rep', 'fsdp')), may hold values from -6 to 6
- frame_ids: int32 [4096], P(('rep', 'fsdp')), may hold values from 0 to 15
- modulation: float32 [16, 6144], replicated, may hold values from -3 to 3
- query_gain: float32 [128], replicated, may hold values from 0.1 to 1.9
- query_weight: bfloat16 [4, 6144, 3072], P('rep', 'fsdp'), may hold values from -0.078125 to 0.078125
- query_cotangent: bfloat16 [4096, 3072], P(('rep', 'fsdp')), may hold values from -6 to 6
- pseudo_grad: float32 [4, 524288], P('rep', 'fsdp'), may hold values from -6 to 6
- outer_params: float32 [524288], P('fsdp'), may hold values from -6 to 6
- outer_momentum: float32 [524288], P('fsdp'), may hold values from -3 to 3
Outputs:
- input_grad: bfloat16 [4096, 6144], P(('rep', 'fsdp'))
- weight_grad: bfloat16 [4, 6144, 3072], P('rep', 'fsdp')
- table_grad: float32 [4, 16, 6144], P('rep', None, 'fsdp')
- new_fragment: float32 [524288], P('fsdp')
- new_momentum: float32 [524288], P('fsdp')
All inputs are finite; a program needn't handle non-finite values.
Results may differ from a plain program's by a relative error of at most 0.02.
Values may be sent and summed in bfloat16 or wider, within the bound.
A program may use at most 128 MiB of HBM per device.

v0:
```python
import jax
import jax.numpy as jnp
from jax import lax
from jax.sharding import PartitionSpec as P

EPSILON = 1e-06
OUTER_RATE = 0.7
OUTER_MOMENTUM = 0.9


def shards(
    clip_tokens,
    frame_ids,
    modulation,
    query_gain,
    query_weight,
    query_cotangent,
    pseudo_grad,
    outer_params,
    outer_momentum,
):
    local_rows = clip_tokens.shape[0]
    tokens_f = clip_tokens.astype(jnp.float32)
    inverse = lax.rsqrt(jnp.mean(tokens_f * tokens_f, axis=-1, keepdims=True) + EPSILON)
    normed = tokens_f * inverse
    frame_count = modulation.shape[0]
    one_hot = (frame_ids[:, None] == jnp.arange(frame_count, dtype=jnp.int32)[None, :]).astype(
        jnp.float32
    )
    frame_mod = jnp.dot(one_hot, modulation, precision=lax.Precision.HIGHEST)
    normal_in = (normed * (1.0 + frame_mod)).astype(jnp.bfloat16)
    gathered_in = lax.all_to_all(normal_in, "fsdp", split_axis=1, concat_axis=0, tiled=True)
    weight_rows = query_weight[0]
    columns = weight_rows.shape[1]
    selected = gathered_in
    projected = lax.psum_scatter(
        jnp.dot(selected, weight_rows, preferred_element_type=jnp.float32).astype(jnp.bfloat16),
        "fsdp",
        scatter_dimension=0,
        tiled=True,
    ).astype(jnp.float32)
    head_size = query_gain.shape[0]
    heads = projected.reshape(local_rows, columns // head_size, head_size)
    head_inv = lax.rsqrt(jnp.mean(heads * heads, axis=-1, keepdims=True) + EPSILON)
    head_hat = heads * head_inv
    scaled = (
        query_cotangent.astype(jnp.float32).reshape(local_rows, columns // head_size, head_size)
        * query_gain
    )
    head_grad = head_inv * (scaled - head_hat * jnp.mean(scaled * head_hat, axis=-1, keepdims=True))
    proj_grad = head_grad.reshape(local_rows, columns).astype(jnp.bfloat16)
    piece = lax.all_gather(proj_grad, "fsdp", axis=0, tiled=True)
    selected = gathered_in
    weight_total = lax.dot_general(
        selected, piece, (((0,), (0,)), ((), ())), preferred_element_type=jnp.float32
    )
    feature_piece = lax.dot_general(
        piece, weight_rows, (((1,), (1,)), ((), ())), preferred_element_type=jnp.float32
    )
    feature_total = feature_piece
    weight_total, feature_total = (weight_total, feature_total)
    weight_grad = weight_total.astype(jnp.bfloat16)[None]
    normal_grad = lax.all_to_all(
        feature_total.astype(jnp.bfloat16), "fsdp", split_axis=0, concat_axis=1, tiled=True
    ).astype(jnp.float32)
    local_table = lax.dot_general(
        one_hot, normal_grad * normed, (((0,), (0,)), ((), ())), precision=lax.Precision.HIGHEST
    )
    table_grad = lax.psum_scatter(
        local_table.astype(jnp.bfloat16), "fsdp", scatter_dimension=1, tiled=True
    ).astype(jnp.float32)[None]
    grad_hat = normal_grad * (1.0 + frame_mod)
    input_grad = (
        inverse * (grad_hat - normed * jnp.mean(grad_hat * normed, axis=-1, keepdims=True))
    ).astype(jnp.bfloat16)
    replicas = lax.axis_size("rep")
    average = lax.psum(pseudo_grad[0].astype(jnp.bfloat16), "rep").astype(jnp.float32) / replicas
    new_momentum = OUTER_MOMENTUM * outer_momentum + average
    new_fragment = outer_params - OUTER_RATE * (average + OUTER_MOMENTUM * new_momentum)
    return (input_grad, weight_grad, table_grad, new_fragment, new_momentum)


def solution(mesh):
    placed = (
        P(("rep", "fsdp"), None),
        P(("rep", "fsdp")),
        P(),
        P(),
        P("rep", "fsdp", None),
        P(("rep", "fsdp"), None),
        P("rep", "fsdp"),
        P("fsdp"),
        P("fsdp"),
    )
    return jax.shard_map(
        shards,
        mesh=mesh,
        in_specs=placed,
        out_specs=(
            P(("rep", "fsdp"), None),
            P("rep", "fsdp", None),
            P("rep", None, "fsdp"),
            P("fsdp"),
            P("fsdp"),
        ),
        check_vma=False,
    )
```

profile of v0, /device:TPU:0, one launch (start us, length us, event | category | flops | bytes accessed | tf_op | source)
XLA Modules:
  0.0 413.8 jit_solution(1752001839073059281)
XLA Ops:
  8.1 1.9 fusion.14
  10.1 4.9 %fusion.8 = (bf16[128,6144]{1,0:T(8,128)(2,1)S(1)}, f32[128,6144]{1,0:T(8,128)}) fusion(bf16[128,6144]{1,0:T(8,128)(2,1)} %param.9, f32[128]{0:T(128)S(1)} %add_rsqrt_fusion.1, f32[16,6144]{1,0:T(8,128)S(1)} %copy-done, s32[128]{0:T(128)} %param.10), kind=kOutput, calls=%fused_computation.14 | convolution fusion | flops 154929152 | bytes 6685696 | tf_op jit(solution)/shard_map/dot_general | solution.py:30
  15.1 44.1 %all_to_all.32 = bf16[128,8,768]{2,0,1:T(8,128)(2,1)S(1)} all-to-all(bf16[128,8,768]{2,0,1:T(8,128)(2,1)S(1)} %bitcast.48), channel_id=1, replica_groups=mesh['rep'=4,'fsdp'=8] {'fsdp'}, dimensions={1} | all-to-all | bytes 3145728 | tf_op jit(solution)/shard_map/all_to_all | solution.py:32
  59.1 1.1 copy-done.5
  60.3 7.0 %convolution_convert_fusion.1 = bf16[1024,3072]{1,0:T(8,128)(2,1)} fusion(bf16[1024,768]{1,0:T(8,128)(2,1)S(1)} %bitcast.52, bf16[1,768,3072]{2,1,0:T(8,128)(2,1)S(1)} %bitcast.56), kind=kOutput, calls=%fused_computation.2 | convolution fusion | flops 4834983936 | bytes 12582912 | tf_op jit(solution)/shard_map/dot_general | solution.py:37
  67.4 1.0 copy-done.3
  68.4 0.1 convert_bitcast_fusion.1
  68.6 0.3 copy.23
  69.0 115.4 %reduce-scatter.3.cloned.1.call-done = bf16[128,3072]{1,0:T(8,128)(2,1)} async-done(((bf16[1024,3072]{1,0:T(8,128)(2,1)}), bf16[128,3072]{1,0:T(8,128)(2,1)}) %reduce-scatter.3.cloned.1.call-update) | async-done | bytes 786448 | tf_op jit(solution)/shard_map/reduce_scatter | solution.py:36
  184.5 1.3 convert_bitcast_fusion.2
  185.8 0.3 copy.21
  186.0 0.5 multiply_reduce_fusion.1
  186.6 1.0 multiply_reduce_fusion
  187.5 0.5 mul.119
  188.0 0.5 mul.108
  188.5 1.8 fusion.21
  190.3 1.3 convert_reduce_fusion
  191.7 96.9 %all-gather.2.cloned.1.call-done = bf16[1024,3072]{1,0:T(8,128)(2,1)} async-done(((bf16[128,3072]{1,0:T(8,128)(2,1)}), bf16[1024,3072]{1,0:T(8,128)(2,1)}) %all-gather.2.cloned.1.call-update) | async-done | bytes 6291472 | tf_op jit(solution)/shard_map/all_gather | solution.py:52
  288.6 9.5 %fusion.15 = bf16[1024,768]{1,0:T(8,128)(2,1)} fusion(bf16[1024,3072]{1,0:T(8,128)(2,1)} %all-gather.2.cloned.1.call-done, bf16[1,768,3072]{2,1,0:T(8,128)(2,1)} %param.13), kind=kOutput, calls=%fused_computation.25 | convolution fusion | flops 4832624640 | bytes 12582912 | tf_op jit(solution)/shard_map/dot_general | solution.py:57
  298.1 3.7 all-to-all-start.1
  301.8 0.2 reduce-scatter.5.cloned.1.call-start
  302.0 2.0 multiply_subtract_fusion
  304.0 9.5 %fusion.3 = bf16[1,768,3072]{2,1,0:T(8,128)(2,1)} fusion(bf16[1024,768]{1,0:T(8,128)(2,1)S(1)} %bitcast.53, bf16[1024,3072]{1,0:T(8,128)(2,1)} %all-gather.2.cloned.1.call-done), kind=kOutput, calls=%fused_computation.7 | convolution fusion | flops 4834197504 | bytes 12582912 | tf_op jit(solution)/shard_map/dot_general | solution.py:54
  313.5 24.9 %all-to-all-done.1 = bf16[8,128,768]{2,1,0:T(8,128)(2,1)S(1)} async-done(((bf16[8,128,768]{2,1,0:T(8,128)(2,1)}), bf16[8,128,768]{2,1,0:T(8,128)(2,1)S(1)}, u32[]{:S(2)}, u32[]{:S(2)}) %all-to-all-start.1) | async-done | bytes 1572896 | tf_op jit(solution)/shard_map/all_to_all | solution.py:63
  338.5 0.3 convert_bitcast_fusion
  338.8 0.3 copy.20
  339.1 1.6 copy-done.2
  340.8 2.2 convolution_convert_fusion
  343.0 5.1 %fusion.9 = (f32[128]{0:T(128)S(1)}, f32[128,6144]{1,0:T(8,128)}) fusion(bf16[128,6144]{1,0:T(8,128)(2,1)S(1)} %copy-done.1, f32[128]{0:T(128)S(1)} %add_rsqrt_fusion.1, f32[128,6144]{1,0:T(8,128)} %bitcast.45, f32[128,6144]{1,0:T(8,128)} %get-tuple-element.10), kind=kLoop, calls=%fused_computation.15 | loop fusion | flops 3932032 | bytes 11011072 | tf_op jit(solution)/shard_map/reduce_sum | solution.py:74
  348.1 3.7 fusion.12
  351.8 53.5 %reduce-scatter.5.cloned.1.call-done = bf16[16,768]{1,0:T(8,128)(2,1)} async-done(((bf16[16,6144]{1,0:T(8,128)(2,1)}), bf16[16,768]{1,0:T(8,128)(2,1)}) %reduce-scatter.5.cloned.1.call-update) | async-done | bytes 24592 | tf_op jit(solution)/shard_map/reduce_scatter | solution.py:69
  405.3 1.4 bitcast_convert_fusion
  (37 shorter events, 0.5 us)
Async XLA Ops:
  8.0 2.0 copy-start
  8.0 176.5 %reduce-scatter.3.cloned.1.call-start = ((), (), s32[]{:S(2)}) async-start(), calls=%async_computation.4 | async-start | bytes 7077888 | tf_op jit(solution)/shard_map/reduce_scatter | solution.py:36
  8.1 52.2 %slice-start = ((s8[4718592]{0:T(1024)(128)(4,1)}), s8[4194304]{0:T(1024)(128)(4,1)S(1)}, s32[]{:S(2)}) async-start(s8[4718592]{0:T(1024)(128)(4,1)} %bitcast.55), calls=%async_computation.8 | async-start | bytes 8388608
  10.0 50.2 %slice-start.1 = ((s8[4718592]{0:T(1024)(128)(4,1)}), s8[524288]{0:T(1024)(128)(4,1)S(1)}, s32[]{:S(2)}) async-start(s8[4718592]{0:T(1024)(128)(4,1)} %bitcast.55), calls=%async_computation.9 | async-start | bytes 1048576
  59.1 1.1 copy-start.5
  67.3 1.1 copy-start.3
  67.3 1.5 copy-start.8
  67.4 221.2 %all-gather.2.cloned.1.call-start = ((), (), s32[]{:S(2)}) async-start(), calls=%async_computation.5 | async-start | bytes 7077888 | tf_op jit(solution)/shard_map/all_gather | solution.py:52
  186.5 1.9 copy-start.4
  188.5 1.8 copy-start.7
  190.3 111.8 %all-reduce.2.cloned.1.call-start = ((), (), s32[]{:S(2)}) async-start(), calls=%async_computation.7 | async-start | bytes 262144 | tf_op jit(solution)/shard_map/psum | solution.py:77
  298.1 5.9 %copy-start.6 = (bf16[128,8,768]{2,0,1:T(8,128)(2,1)S(1)}, bf16[128,8,768]{2,0,1:T(8,128)(2,1)}, u32[]{:S(2)}) copy-start(bf16[128,8,768]{2,0,1:T(8,128)(2,1)} %copy-done.5) | copy-start | bytes 4718596
  298.1 40.4 %all-to-all-start.1 = ((bf16[8,128,768]{2,1,0:T(8,128)(2,1)}), bf16[8,128,768]{2,1,0:T(8,128)(2,1)S(1)}, u32[]{:S(2)}, u32[]{:S(2)}) async-start(bf16[8,128,768]{2,1,0:T(8,128)(2,1)} %bitcast.54), calls=%async_computation.2 | async-start | bytes 3145728 | tf_op jit(solution)/shard_map/all_to_all | solution.py:63
  301.8 103.5 %reduce-scatter.5.cloned.1.call-start = ((), (), s32[]{:S(2)}) async-start(), calls=%async_computation.6 | async-start | bytes 221184 | tf_op jit(solution)/shard_map/reduce_scatter | solution.py:69
  338.7 2.0 copy-start.1
  338.8 2.0 copy-start.9
  339.1 1.6 copy-start.2
Sparse Core Ops, SparseCore 0:
  67.5 116.9 reduce-scatter.2
  190.4 98.1 all-gather.1
  348.2 57.0 reduce-scatter.4
Sparse Core Ops, SparseCore 1:
  193.7 30.5 all-reduce.1
where the time goes:
time: 414 us
  waiting for transfers between devices  291 us (70%)
  blocking collectives  44.1 us (11%)
  matrix products  33.2 us (8%)
  other arithmetic  20.4 us (5%)
  between operations  15.4 us (4%)
  local copies, waits for them, and re-layouts  5.82 us (1%)
    reduce_scatter x1, waiting for transfers between devices, shards(): lax.psum_scatter(jnp.dot(selected, weight_rows, preferred_element_type=jn...  115 us
    all_gather x1, waiting for transfers between devices, shards(): piece = lax.all_gather(proj_grad, 'fsdp', axis=0, tiled=True)  96.9 us
    reduce_scatter x1, waiting for transfers between devices, shards(): lax.psum_scatter(local_table.astype(jnp.bfloat16), 'fsdp', scatter_dimens...  53.5 us
    all_to_all x1, blocking collectives, shards(): lax.all_to_all(normal_in, 'fsdp', split_axis=1, concat_axis=0, tiled=True)  44.1 us
    all_to_all x1, waiting for transfers between devices, shards(): lax.all_to_all(feature_total.astype(jnp.bfloat16), 'fsdp', split_axis=0,...  24.9 us
    dot_general x1, matrix products, shards(): lax.dot_general(selected, piece, (((0,), (0,)), ((), ())), preferred_elem...  9.54 us
    dot_general x1, matrix products, shards(): lax.dot_general(piece, weight_rows, (((1,), (1,)), ((), ())), preferred_e...  9.47 us
  transfers between devices with their start and end apart: 5, of which 4 were waited for; matrix products, arithmetic and copies ran while one was open for 6% of the time, Pallas kernels for 0%

commit v1 on v0

v1 whole, which is shorter than its diff:
```python
import jax
import jax.numpy as jnp
from jax import lax
from jax.sharding import PartitionSpec as P

EPSILON = 1e-06
OUTER_RATE = 0.7
OUTER_MOMENTUM = 0.9
CHUNKS = 4


def shards(
    clip_tokens,
    frame_ids,
    modulation,
    query_gain,
    query_weight,
    query_cotangent,
    pseudo_grad,
    outer_params,
    outer_momentum,
):
    n = lax.axis_size("fsdp")
    me = lax.axis_index("fsdp")
    rows, width = clip_tokens.shape
    part = width // n
    weight_rows = query_weight[0]
    columns = weight_rows.shape[1]
    head_size = query_gain.shape[0]
    frame_count = modulation.shape[0]
    f32 = jnp.float32

    def swap(value, k):
        return lax.ppermute(value, "fsdp", [(i, i ^ k) for i in range(n)])

    def column_block(value, k):
        return lax.dynamic_slice_in_dim(value, (me ^ k) * part, part, 1)

    tokens_all = jnp.concatenate(
        [column_block(clip_tokens, 0)] + [swap(column_block(clip_tokens, k), k) for k in range(1, n)], 0
    )
    tokens_f = clip_tokens.astype(f32)
    inverse = lax.rsqrt(jnp.mean(tokens_f * tokens_f, axis=-1, keepdims=True) + EPSILON)
    sides = jnp.stack([inverse[:, 0], frame_ids.astype(f32)])
    sides_all = lax.all_gather(sides, "fsdp", axis=0)
    sides_all = jnp.stack([lax.dynamic_index_in_dim(sides_all, me ^ k, 0, False) for k in range(n)])
    inverse_all = sides_all[:, 0].reshape(n * rows, 1)
    frames_all = sides_all[:, 1].reshape(n * rows, 1)
    one_hot_all = (frames_all == jnp.arange(frame_count, dtype=f32)[None, :]).astype(f32)
    normed_all = tokens_all.astype(f32) * inverse_all
    mod_all = jnp.dot(one_hot_all, column_block(modulation, 0), precision=lax.Precision.HIGHEST)
    normal_in = (normed_all * (1.0 + mod_all)).astype(jnp.bfloat16)

    chunk = columns // CHUNKS
    weight_parts = []
    feature_total = jnp.zeros((n * rows, part), f32)
    for c in range(CHUNKS):
        weight_c = weight_rows[:, c * chunk : (c + 1) * chunk]
        partial = jnp.dot(normal_in, weight_c, preferred_element_type=f32).astype(jnp.bfloat16)
        partial = partial.reshape(n // 2, 2, rows, chunk)
        pair = partial[:, 0].astype(f32) + swap(partial[:, 1], 1).astype(f32)
        pair_sent = pair.astype(jnp.bfloat16)
        projected = pair[0]
        for k in range(1, n // 2):
            projected = projected + swap(pair_sent[k], 2 * k).astype(f32)
        heads = projected.reshape(rows, chunk // head_size, head_size)
        head_inv = lax.rsqrt(jnp.mean(heads * heads, axis=-1, keepdims=True) + EPSILON)
        head_hat = heads * head_inv
        cotangent = query_cotangent[:, c * chunk : (c + 1) * chunk].astype(f32)
        scaled = cotangent.reshape(heads.shape) * query_gain
        head_grad = head_inv * (
            scaled - head_hat * jnp.mean(scaled * head_hat, axis=-1, keepdims=True)
        )
        proj_grad = head_grad.reshape(rows, chunk).astype(jnp.bfloat16)
        line = jnp.stack([proj_grad] + [swap(proj_grad, 2 * k) for k in range(1, n // 2)])
        piece = jnp.stack([line, swap(line, 1)], axis=1).reshape(n * rows, chunk)
        weight_parts.append(
            lax.dot_general(
                normal_in, piece, (((0,), (0,)), ((), ())), preferred_element_type=f32
            ).astype(jnp.bfloat16)
        )
        feature_total = feature_total + lax.dot_general(
            piece, weight_c, (((1,), (1,)), ((), ())), preferred_element_type=f32
        )
    weight_grad = jnp.concatenate(weight_parts, axis=1)[None]
    feature = feature_total.astype(jnp.bfloat16)
    table_grad = lax.dot_general(
        one_hot_all,
        feature.astype(f32) * normed_all,
        (((0,), (0,)), ((), ())),
        precision=lax.Precision.HIGHEST,
    )[None]

    blocks = feature.reshape(n, rows, part)
    normal_grad = jnp.zeros((rows, width), jnp.bfloat16)
    for k in range(n):
        arrived = blocks[0] if k == 0 else swap(blocks[k], k)
        normal_grad = lax.dynamic_update_slice_in_dim(normal_grad, arrived, (me ^ k) * part, 1)
    normal_grad = normal_grad.astype(f32)
    normed = tokens_f * inverse
    one_hot = (frame_ids[:, None] == jnp.arange(frame_count, dtype=jnp.int32)[None, :]).astype(f32)
    frame_mod = jnp.dot(one_hot, modulation, precision=lax.Precision.HIGHEST)
    grad_hat = normal_grad * (1.0 + frame_mod)
    input_grad = (
        inverse * (grad_hat - normed * jnp.mean(grad_hat * normed, axis=-1, keepdims=True))
    ).astype(jnp.bfloat16)
    replicas = lax.axis_size("rep")
    average = lax.psum(pseudo_grad[0].astype(jnp.bfloat16), "rep").astype(f32) / replicas
    new_momentum = OUTER_MOMENTUM * outer_momentum + average
    new_fragment = outer_params - OUTER_RATE * (average + OUTER_MOMENTUM * new_momentum)
    return (input_grad, weight_grad, table_grad, new_fragment, new_momentum)


def solution(mesh):
    placed = (
        P(("rep", "fsdp"), None),
        P(("rep", "fsdp")),
        P(),
        P(),
        P("rep", "fsdp", None),
        P(("rep", "fsdp"), None),
        P("rep", "fsdp"),
        P("fsdp"),
        P("fsdp"),
    )
    return jax.shard_map(
        shards,
        mesh=mesh,
        in_specs=placed,
        out_specs=(
            P(("rep", "fsdp"), None),
            P("rep", "fsdp", None),
            P("rep", None, "fsdp"),
            P("fsdp"),
            P("fsdp"),
        ),
        check_vma=False,
    )
```

time: 414 us -> 408 us (0.986); the launches traced: 414 us -> 401 us
  waiting for transfers between devices: 291 us -> 114 us
  starting transfers between devices: 4.06 us -> 112 us
  local copies, waits for them, and re-layouts: 5.82 us -> 58 us
  blocking collectives: 44.1 us -> 26.6 us
  matrix products: 33.2 us -> 44.8 us
  other arithmetic: 20.4 us -> 30.8 us
    reduce_scatter x2 -> x0, waiting for transfers between devices: 169 us -> none  [the longest x1 115 us: shards(): lax.psum_scatter(jnp.dot(selected, weight_rows, preferred_element_type=jn...]
    ppermute x0 -> x46, waiting for transfers between devices: none -> 114 us  [swap(): return lax.ppermute(value, 'fsdp', [(i, i ^ k) for i in range(n)])]
    ppermute x0 -> x46, starting transfers between devices: none -> 112 us  [swap(): return lax.ppermute(value, 'fsdp', [(i, i ^ k) for i in range(n)])]
    all_gather x1 -> x0, waiting for transfers between devices: 96.9 us -> none  [shards(): piece = lax.all_gather(proj_grad, 'fsdp', axis=0, tiled=True)]
    all_to_all x1 -> x0, blocking collectives: 44.1 us -> none  [shards(): lax.all_to_all(normal_in, 'fsdp', split_axis=1, concat_axis=0, tiled=True)]
    unnamed x26 -> x106, local copies, waits for them, and re-layouts: 4.44 us -> 35.1 us
    all_gather x0 -> x1, blocking collectives: none -> 26.6 us  [shards(): sides_all = lax.all_gather(sides, 'fsdp', axis=0)]
    all_to_all x1 -> x0, waiting for transfers between devices: 24.9 us -> none  [shards(): lax.all_to_all(feature_total.astype(jnp.bfloat16), 'fsdp', split_axis=0,...]
  transfers between devices with their start and end apart: 5 -> 47, of which waited for: 4 -> 18; matrix products, arithmetic and copies ran while one was open for 6% -> 26% of each run, Pallas kernels for 0% -> 0%
where the time goes in v1:
time: 408 us; the launch traced here: 401 us
  waiting for transfers between devices  114 us (28%)
  starting transfers between devices  112 us (27%)
  local copies, waits for them, and re-layouts  58 us (14%)
  matrix products  44.8 us (11%)
  other arithmetic  30.8 us (8%)
  blocking collectives  26.6 us (7%)
  between operations  14.9 us (4%)
    ppermute x46, waiting for transfers between devices, swap(): return lax.ppermute(value, 'fsdp', [(i, i ^ k) for i in range(n)])  114 us
    ppermute x46, starting transfers between devices, swap(): return lax.ppermute(value, 'fsdp', [(i, i ^ k) for i in range(n)])  112 us
    unnamed x106, local copies, waits for them, and re-layouts  35.1 us
    all_gather x1, blocking collectives, shards(): sides_all = lax.all_gather(sides, 'fsdp', axis=0)  26.6 us
    dot_general x4, matrix products, shards(): lax.dot_general(piece, weight_c, (((1,), (1,)), ((), ())), preferred_elem...  17.9 us
    another operation x8, other arithmetic, shards(): piece = jnp.stack([line, swap(line, 1)], axis=1).reshape(n * rows, chunk)  15.5 us
    dot_general x4, matrix products, shards(): lax.dot_general(normal_in, piece, (((0,), (0,)), ((), ())), preferred_ele...  11.2 us
    dot_general x4, matrix products, shards(): jnp.dot(normal_in, weight_c, preferred_element_type=f32)  9.68 us
  transfers between devices with their start and end apart: 47, of which 18 were waited for; matrix products, arithmetic and copies ran while one was open for 26% of the time, Pallas kernels for 0%

profile of v1, /device:TPU:0, one launch (start us, length us, event | category | flops | bytes accessed | tf_op | source)
XLA Modules:
  0.0 401.3 jit_solution(17984641496850352583)
XLA Ops:
  19.2 26.6 %all-gather.1 = f32[8,2,128]{2,1,0:T(2,128)S(1)} all-gather(f32[1,2,128]{2,1,0:T(2,128)S(1)} %maximum_bitcast_fusion.1), channel_id=2, replica_groups=mesh['rep'=4,'fsdp'=8] {'fsdp'}, dimensions={0}, use_global_device_ids=true | all-gather | bytes 9216 | tf_op jit(solution)/shard_map/all_gather | solution.py:45
  103.8 3.9 collective-permute-start.10
  107.7 3.2 collective-permute-start.8
  110.9 6.9 %collective-permute-done.23 = bf16[4,128,768]{1,2,0:T(8,128)(2,1)} collective-permute-done((bf16[4,128,768]{1,2,0:T(8,128)(2,1)}, bf16[4,128,768]{1,2,0:T(8,128)(2,1)}, u32[]{:S(2)}, u32[]{:S(2)}) %collective-permute-start.23) | collective-permute-done | bytes 786464 | tf_op jit(solution)/shard_map/ppermute | solution.py:34
  117.8 6.5 %collective-permute-start.9 = (bf16[128,768]{0,1:T(8,128)(2,1)S(1)}, bf16[128,768]{0,1:T(8,128)(2,1)S(1)}, u32[]{:S(2)}, u32[]{:S(2)}) collective-permute-start(bf16[128,768]{0,1:T(8,128)(2,1)S(1)} %get-tuple-element.72), channel_id=1, source_target_pairs={{0,4},{1,5},{2,6},{3,7},{4,0},{5,1},{6,2},{7,3},{8,12},{9,13},{10,... | collective-permute-start | bytes 589832 | tf_op jit(solution)/shard_map/ppermute | solution.py:34
  125.7 9.0 %collective-permute-done.15 = bf16[4,128,768]{1,2,0:T(8,128)(2,1)} collective-permute-done((bf16[4,128,768]{1,2,0:T(8,128)(2,1)}, bf16[4,128,768]{1,2,0:T(8,128)(2,1)}, u32[]{:S(2)}, u32[]{:S(2)}) %collective-permute-start.15) | collective-permute-done | bytes 786464 | tf_op jit(solution)/shard_map/ppermute | solution.py:34
  134.6 5.9 %collective-permute-start.24 = (bf16[128,768]{0,1:T(8,128)(2,1)S(1)}, bf16[128,768]{0,1:T(8,128)(2,1)S(1)}, u32[]{:S(2)}, u32[]{:S(2)}) collective-permute-start(bf16[128,768]{0,1:T(8,128)(2,1)S(1)} %get-tuple-element.79), channel_id=1, source_target_pairs={{0,2},{1,3},{2,0},{3,1},{4,6},{5,7},{6,4},{7,5},{8,10},{9,11},{10,... | collective-permute-start | bytes 589832 | tf_op jit(solution)/shard_map/ppermute | solution.py:34
  145.1 7.7 %collective-permute-start.25 = (bf16[128,768]{0,1:T(8,128)(2,1)S(1)}, bf16[128,768]{0,1:T(8,128)(2,1)S(1)}, u32[]{:S(2)}, u32[]{:S(2)}) collective-permute-start(bf16[128,768]{0,1:T(8,128)(2,1)S(1)} %get-tuple-element.81), channel_id=1, source_target_pairs={{0,4},{1,5},{2,6},{3,7},{4,0},{5,1},{6,2},{7,3},{8,12},{9,13},{10,... | collective-permute-start | bytes 589832 | tf_op jit(solution)/shard_map/ppermute | solution.py:34
  154.2 3.6 collective-permute-start.26
  158.8 3.6 collective-permute-start.18
  162.4 8.1 %collective-permute-done.25 = bf16[128,768]{0,1:T(8,128)(2,1)S(1)} collective-permute-done((bf16[128,768]{0,1:T(8,128)(2,1)S(1)}, bf16[128,768]{0,1:T(8,128)(2,1)S(1)}, u32[]{:S(2)}, u32[]{:S(2)}) %collective-permute-start.25) | collective-permute-done | bytes 196640 | tf_op jit(solution)/shard_map/ppermute | solution.py:34
  170.5 12.4 %collective-permute-start.33 = (bf16[128,768]{0,1:T(8,128)(2,1)S(1)}, bf16[128,768]{0,1:T(8,128)(2,1)S(1)}, u32[]{:S(2)}, u32[]{:S(2)}) collective-permute-start(bf16[128,768]{0,1:T(8,128)(2,1)S(1)} %get-tuple-element.78), channel_id=1, source_target_pairs={{0,4},{1,5},{2,6},{3,7},{4,0},{5,1},{6,2},{7,3},{8,12},{9,13},{10,... | collective-permute-start | bytes 589832 | tf_op jit(solution)/shard_map/ppermute | solution.py:34
  183.0 3.3 collective-permute-start.34
  187.7 12.3 %collective-permute-done.33 = bf16[128,768]{0,1:T(8,128)(2,1)S(1)} collective-permute-done((bf16[128,768]{0,1:T(8,128)(2,1)S(1)}, bf16[128,768]{0,1:T(8,128)(2,1)S(1)}, u32[]{:S(2)}, u32[]{:S(2)}) %collective-permute-start.33) | collective-permute-done | bytes 196640 | tf_op jit(solution)/shard_map/ppermute | solution.py:34
  208.1 5.4 %collective-permute-done.19 = bf16[128,768]{0,1:T(8,128)(2,1)S(1)} collective-permute-done((bf16[128,768]{0,1:T(8,128)(2,1)S(1)}, bf16[128,768]{0,1:T(8,128)(2,1)S(1)}, u32[]{:S(2)}, u32[]{:S(2)}) %collective-permute-start.19) | collective-permute-done | bytes 196640 | tf_op jit(solution)/shard_map/ppermute | solution.py:34
  215.5 5.5 %collective-permute-done.20 = bf16[128,768]{0,1:T(8,128)(2,1)S(1)} collective-permute-done((bf16[128,768]{0,1:T(8,128)(2,1)S(1)}, bf16[128,768]{0,1:T(8,128)(2,1)S(1)}, u32[]{:S(2)}, u32[]{:S(2)}) %collective-permute-start.20) | collective-permute-done | bytes 196640 | tf_op jit(solution)/shard_map/ppermute | solution.py:34
  221.1 12.7 %collective-permute-start.36 = (bf16[128,768]{0,1:T(8,128)(2,1)S(1)}, bf16[128,768]{0,1:T(8,128)(2,1)S(1)}, u32[]{:S(2)}, u32[]{:S(2)}) collective-permute-start(bf16[128,768]{0,1:T(8,128)(2,1)S(1)} %get-tuple-element.84), channel_id=1, source_target_pairs={{0,4},{1,5},{2,6},{3,7},{4,0},{5,1},{6,2},{7,3},{8,12},{9,13},{10,... | collective-permute-start | bytes 589832 | tf_op jit(solution)/shard_map/ppermute | solution.py:34
  238.3 5.8 %collective-permute-done.12 = bf16[128,768]{0,1:T(8,128)(2,1)} collective-permute-done((bf16[128,768]{0,1:T(8,128)(2,1)S(1)}, bf16[128,768]{0,1:T(8,128)(2,1)}, u32[]{:S(2)}, u32[]{:S(2)}) %collective-permute-start.12) | collective-permute-done | bytes 196640 | tf_op jit(solution)/shard_map/ppermute | solution.py:34
  244.2 6.2 %collective-permute-start.28 = (bf16[128,768]{0,1:T(8,128)(2,1)S(1)}, bf16[128,768]{0,1:T(8,128)(2,1)}, u32[]{:S(2)}, u32[]{:S(2)}) collective-permute-start(bf16[128,768]{0,1:T(8,128)(2,1)S(1)} %get-tuple-element.86), channel_id=1, source_target_pairs={{0,4},{1,5},{2,6},{3,7},{4,0},{5,1},{6,2},{7,3},{8,12},{9,13},{10,... | collective-permute-start | bytes 589832 | tf_op jit(solution)/shard_map/ppermute | solution.py:34
  253.6 7.3 %collective-permute-done.36 = bf16[128,768]{0,1:T(8,128)(2,1)S(1)} collective-permute-done((bf16[128,768]{0,1:T(8,128)(2,1)S(1)}, bf16[128,768]{0,1:T(8,128)(2,1)S(1)}, u32[]{:S(2)}, u32[]{:S(2)}) %collective-permute-start.36) | collective-permute-done | bytes 196640 | tf_op jit(solution)/shard_map/ppermute | solution.py:34
  272.7 8.8 %collective-permute-done.22 = bf16[4,128,768]{1,2,0:T(8,128)(2,1)} collective-permute-done((bf16[4,128,768]{1,2,0:T(8,128)(2,1)S(1)}, bf16[4,128,768]{1,2,0:T(8,128)(2,1)}, u32[]{:S(2)}, u32[]{:S(2)}) %collective-permute-start.22) | collective-permute-done | bytes 786464 | tf_op jit(solution)/shard_map/ppermute | solution.py:34
  282.9 15.5 %collective-permute-done.14 = bf16[4,128,768]{1,2,0:T(8,128)(2,1)} collective-permute-done((bf16[4,128,768]{1,2,0:T(8,128)(2,1)}, bf16[4,128,768]{1,2,0:T(8,128)(2,1)}, u32[]{:S(2)}, u32[]{:S(2)}) %collective-permute-start.14) | collective-permute-done | bytes 786464 | tf_op jit(solution)/shard_map/ppermute | solution.py:34
  305.1 4.5 %fusion.19 = f32[1024,768]{1,0:T(8,128)} fusion(bf16[1024,768]{1,0:T(8,128)(2,1)S(1)} %bitcast.233, bf16[768,3072]{1,0:T(8,128)(2,1)} %bitcast.244), kind=kOutput, calls=%fused_computation.41 | convolution fusion | flops 1207959552 | bytes 5898240 | tf_op jit(solution)/shard_map/dot_general | solution.py:82
  312.2 8.2 %collective-permute-done.30 = bf16[4,128,768]{1,2,0:T(8,128)(2,1)} collective-permute-done((bf16[4,128,768]{1,2,0:T(8,128)(2,1)}, bf16[4,128,768]{1,2,0:T(8,128)(2,1)}, u32[]{:S(2)}, u32[]{:S(2)}) %collective-permute-start.30) | collective-permute-done | bytes 786464 | tf_op jit(solution)/shard_map/ppermute | solution.py:34
  323.2 5.0 %fusion.22 = f32[1024,768]{1,0:T(8,128)} fusion(bf16[1024,768]{1,0:T(8,128)(2,1)} %bitcast.227, bf16[768,3072]{1,0:T(8,128)(2,1)} %bitcast.245), kind=kOutput, calls=%fused_computation.44 | convolution fusion | flops 1207959552 | bytes 5898240 | tf_op jit(solution)/shard_map/dot_general | solution.py:82
  328.3 4.5 %fusion.16 = f32[1024,768]{1,0:T(8,128)} fusion(bf16[1024,768]{1,0:T(8,128)(2,1)S(1)} %bitcast.230, bf16[768,3072]{1,0:T(8,128)(2,1)} %bitcast.246), kind=kOutput, calls=%fused_computation.38 | convolution fusion | flops 1207959552 | bytes 5898240 | tf_op jit(solution)/shard_map/dot_general | solution.py:82
  340.8 3.5 convolution_convert_fusion.4
  345.1 3.9 add_convert_fusion
  350.5 3.1 collective-permute-start.40
  358.5 6.6 %copy.68 = bf16[1,768,3072]{2,1,0:T(8,128)(2,1)} copy(bf16[1,768,3072]{1,2,0:T(8,128)(2,1)} %maximum_bitcast_fusion) | data formatting | bytes 9437184
  376.8 9.3 %collective-permute-done.42 = bf16[128,768]{1,0:T(8,128)(2,1)S(1)} collective-permute-done((bf16[128,768]{1,0:T(8,128)(2,1)}, bf16[128,768]{1,0:T(8,128)(2,1)S(1)}, u32[]{:S(2)}, u32[]{:S(2)}) %collective-permute-start.42) | collective-permute-done | bytes 196640 | tf_op jit(solution)/shard_map/ppermute | solution.py:34
  386.1 4.0 collective-permute-done.43
  (249 shorter events, 153.7 us)
Async XLA Ops:
  7.2 256.5 %all-reduce.2.cloned.1.call-start = ((), (), s32[]{:S(2)}) async-start(), calls=%async_computation | async-start | bytes 262144 | tf_op jit(solution)/shard_map/psum | solution.py:108
  10.0 51.0 %collective-permute-start = (bf16[128,768]{1,0:T(8,128)(2,1)}, bf16[128,768]{1,0:T(8,128)(2,1)}, u32[]{:S(2)}, u32[]{:S(2)}) collective-permute-start(bf16[128,768]{1,0:T(8,128)(2,1)} %get-tuple-element.55), channel_id=1, source_target_pairs={{0,1},{1,0},{2,3},{3,2},{4,5},{5,4},{6,7},{7,6},{8,9},{9,8},{10,11... | collective-permute-start | bytes 589832 | tf_op jit(solution)/shard_map/ppermute | solution.py:34
  12.9 49.0 %collective-permute-start.1 = (bf16[128,768]{1,0:T(8,128)(2,1)}, bf16[128,768]{1,0:T(8,128)(2,1)}, u32[]{:S(2)}, u32[]{:S(2)}) collective-permute-start(bf16[128,768]{1,0:T(8,128)(2,1)} %get-tuple-element.54), channel_id=1, source_target_pairs={{0,2},{1,3},{2,0},{3,1},{4,6},{5,7},{6,4},{7,5},{8,10},{9,11},{10,... | collective-permute-start | bytes 589832 | tf_op jit(solution)/shard_map/ppermute | solution.py:34
  14.5 51.4 %collective-permute-start.2 = (bf16[128,768]{1,0:T(8,128)(2,1)}, bf16[128,768]{1,0:T(8,128)(2,1)}, u32[]{:S(2)}, u32[]{:S(2)}) collective-permute-start(bf16[128,768]{1,0:T(8,128)(2,1)} %get-tuple-element.53), channel_id=1, source_target_pairs={{0,3},{1,2},{2,1},{3,0},{4,7},{5,6},{6,5},{7,4},{8,11},{9,10},{10,... | collective-permute-start | bytes 589832 | tf_op jit(solution)/shard_map/ppermute | solution.py:34
  14.5 52.4 %collective-permute-start.3 = (bf16[128,768]{1,0:T(8,128)(2,1)}, bf16[128,768]{1,0:T(8,128)(2,1)}, u32[]{:S(2)}, u32[]{:S(2)}) collective-permute-start(bf16[128,768]{1,0:T(8,128)(2,1)} %get-tuple-element.52), channel_id=1, source_target_pairs={{0,4},{1,5},{2,6},{3,7},{4,0},{5,1},{6,2},{7,3},{8,12},{9,13},{10,... | collective-permute-start | bytes 589832 | tf_op jit(solution)/shard_map/ppermute | solution.py:34
  17.5 50.5 %collective-permute-start.4 = (bf16[128,768]{1,0:T(8,128)(2,1)}, bf16[128,768]{1,0:T(8,128)(2,1)}, u32[]{:S(2)}, u32[]{:S(2)}) collective-permute-start(bf16[128,768]{1,0:T(8,128)(2,1)} %get-tuple-element.51), channel_id=1, source_target_pairs={{0,5},{1,4},{2,7},{3,6},{4,1},{5,0},{6,3},{7,2},{8,13},{9,12},{10,... | collective-permute-start | bytes 589832 | tf_op jit(solution)/shard_map/ppermute | solution.py:34
  80.1 22.0 %collective-permute-start.7 = (bf16[4,128,768]{1,2,0:T(8,128)(2,1)}, bf16[4,128,768]{1,2,0:T(8,128)(2,1)}, u32[]{:S(2)}, u32[]{:S(2)}) collective-permute-start(bf16[4,128,768]{1,2,0:T(8,128)(2,1)} %bitcast.242), channel_id=1, source_target_pairs={{0,1},{1,0},{2,3},{3,2},{4,5},{5,4},{6,7},{7,6},{8,9},{9,8},{10,11... | collective-permute-start | bytes 2359304 | tf_op jit(solution)/shard_map/ppermute | solution.py:34
  86.6 31.2 %collective-permute-start.23 = (bf16[4,128,768]{1,2,0:T(8,128)(2,1)}, bf16[4,128,768]{1,2,0:T(8,128)(2,1)}, u32[]{:S(2)}, u32[]{:S(2)}) collective-permute-start(bf16[4,128,768]{1,2,0:T(8,128)(2,1)} %bitcast.241), channel_id=1, source_target_pairs={{0,1},{1,0},{2,3},{3,2},{4,5},{5,4},{6,7},{7,6},{8,9},{9,8},{10,11... | collective-permute-start | bytes 2359304 | tf_op jit(solution)/shard_map/ppermute | solution.py:34
  94.1 40.5 %collective-permute-start.15 = (bf16[4,128,768]{1,2,0:T(8,128)(2,1)}, bf16[4,128,768]{1,2,0:T(8,128)(2,1)}, u32[]{:S(2)}, u32[]{:S(2)}) collective-permute-start(bf16[4,128,768]{1,2,0:T(8,128)(2,1)} %bitcast.27), channel_id=1, source_target_pairs={{0,1},{1,0},{2,3},{3,2},{4,5},{5,4},{6,7},{7,6},{8,9},{9,8},{10,11... | collective-permute-start | bytes 2359304 | tf_op jit(solution)/shard_map/ppermute | solution.py:34
  101.5 43.6 %collective-permute-start.31 = (bf16[4,128,768]{1,2,0:T(8,128)(2,1)}, bf16[4,128,768]{1,2,0:T(8,128)(2,1)}, u32[]{:S(2)}, u32[]{:S(2)}) collective-permute-start(bf16[4,128,768]{1,2,0:T(8,128)(2,1)} %bitcast.240), channel_id=1, source_target_pairs={{0,1},{1,0},{2,3},{3,2},{4,5},{5,4},{6,7},{7,6},{8,9},{9,8},{10,11... | collective-permute-start | bytes 2359304 | tf_op jit(solution)/shard_map/ppermute | solution.py:34
  103.8 50.4 %collective-permute-start.10 = (bf16[128,768]{0,1:T(8,128)(2,1)S(1)}, bf16[128,768]{0,1:T(8,128)(2,1)S(1)}, u32[]{:S(2)}, u32[]{:S(2)}) collective-permute-start(bf16[128,768]{0,1:T(8,128)(2,1)S(1)} %get-tuple-element.71), channel_id=1, source_target_pairs={{0,6},{1,7},{2,4},{3,5},{4,2},{5,3},{6,0},{7,1},{8,14},{9,15},{10,... | collective-permute-start | bytes 589832 | tf_op jit(solution)/shard_map/ppermute | solution.py:34
  107.7 50.1 %collective-permute-start.8 = (bf16[128,768]{0,1:T(8,128)(2,1)S(1)}, bf16[128,768]{0,1:T(8,128)(2,1)S(1)}, u32[]{:S(2)}, u32[]{:S(2)}) collective-permute-start(bf16[128,768]{0,1:T(8,128)(2,1)S(1)} %get-tuple-element.70), channel_id=1, source_target_pairs={{0,2},{1,3},{2,0},{3,1},{4,6},{5,7},{6,4},{7,5},{8,10},{9,11},{10,... | collective-permute-start | bytes 589832 | tf_op jit(solution)/shard_map/ppermute | solution.py:34
  117.8 40.0 %collective-permute-start.9 = (bf16[128,768]{0,1:T(8,128)(2,1)S(1)}, bf16[128,768]{0,1:T(8,128)(2,1)S(1)}, u32[]{:S(2)}, u32[]{:S(2)}) collective-permute-start(bf16[128,768]{0,1:T(8,128)(2,1)S(1)} %get-tuple-element.72), channel_id=1, source_target_pairs={{0,4},{1,5},{2,6},{3,7},{4,0},{5,1},{6,2},{7,3},{8,12},{9,13},{10,... | collective-permute-start | bytes 589832 | tf_op jit(solution)/shard_map/ppermute | solution.py:34
  134.6 24.2 %collective-permute-start.24 = (bf16[128,768]{0,1:T(8,128)(2,1)S(1)}, bf16[128,768]{0,1:T(8,128)(2,1)S(1)}, u32[]{:S(2)}, u32[]{:S(2)}) collective-permute-start(bf16[128,768]{0,1:T(8,128)(2,1)S(1)} %get-tuple-element.79), channel_id=1, source_target_pairs={{0,2},{1,3},{2,0},{3,1},{4,6},{5,7},{6,4},{7,5},{8,10},{9,11},{10,... | collective-permute-start | bytes 589832 | tf_op jit(solution)/shard_map/ppermute | solution.py:34
  145.1 25.4 %collective-permute-start.25 = (bf16[128,768]{0,1:T(8,128)(2,1)S(1)}, bf16[128,768]{0,1:T(8,128)(2,1)S(1)}, u32[]{:S(2)}, u32[]{:S(2)}) collective-permute-start(bf16[128,768]{0,1:T(8,128)(2,1)S(1)} %get-tuple-element.81), channel_id=1, source_target_pairs={{0,4},{1,5},{2,6},{3,7},{4,0},{5,1},{6,2},{7,3},{8,12},{9,13},{10,... | collective-permute-start | bytes 589832 | tf_op jit(solution)/shard_map/ppermute | solution.py:34
  157.8 25.2 %collective-permute-start.16 = (bf16[128,768]{0,1:T(8,128)(2,1)S(1)}, bf16[128,768]{0,1:T(8,128)(2,1)S(1)}, u32[]{:S(2)}, u32[]{:S(2)}) collective-permute-start(bf16[128,768]{0,1:T(8,128)(2,1)S(1)} %get-tuple-element.73), channel_id=1, source_target_pairs={{0,2},{1,3},{2,0},{3,1},{4,6},{5,7},{6,4},{7,5},{8,10},{9,11},{10,... | collective-permute-start | bytes 589832 | tf_op jit(solution)/shard_map/ppermute | solution.py:34
  157.8 29.5 %collective-permute-start.17 = (bf16[128,768]{0,1:T(8,128)(2,1)S(1)}, bf16[128,768]{0,1:T(8,128)(2,1)S(1)}, u32[]{:S(2)}, u32[]{:S(2)}) collective-permute-start(bf16[128,768]{0,1:T(8,128)(2,1)S(1)} %get-tuple-element.75), channel_id=1, source_target_pairs={{0,4},{1,5},{2,6},{3,7},{4,0},{5,1},{6,2},{7,3},{8,12},{9,13},{10,... | collective-permute-start | bytes 589832 | tf_op jit(solution)/shard_map/ppermute | solution.py:34
  158.8 28.5 %collective-permute-start.18 = (bf16[128,768]{0,1:T(8,128)(2,1)S(1)}, bf16[128,768]{0,1:T(8,128)(2,1)S(1)}, u32[]{:S(2)}, u32[]{:S(2)}) collective-permute-start(bf16[128,768]{0,1:T(8,128)(2,1)S(1)} %get-tuple-element.74), channel_id=1, source_target_pairs={{0,6},{1,7},{2,4},{3,5},{4,2},{5,3},{6,0},{7,1},{8,14},{9,15},{10,... | collective-permute-start | bytes 589832 | tf_op jit(solution)/shard_map/ppermute | solution.py:34
  170.5 29.5 %collective-permute-start.33 = (bf16[128,768]{0,1:T(8,128)(2,1)S(1)}, bf16[128,768]{0,1:T(8,128)(2,1)S(1)}, u32[]{:S(2)}, u32[]{:S(2)}) collective-permute-start(bf16[128,768]{0,1:T(8,128)(2,1)S(1)} %get-tuple-element.78), channel_id=1, source_target_pairs={{0,4},{1,5},{2,6},{3,7},{4,0},{5,1},{6,2},{7,3},{8,12},{9,13},{10,... | collective-permute-start | bytes 589832 | tf_op jit(solution)/shard_map/ppermute | solution.py:34
  206.2 27.6 %collective-permute-start.11 = (bf16[128,768]{0,1:T(8,128)(2,1)S(1)}, bf16[128,768]{0,1:T(8,128)(2,1)S(1)}, u32[]{:S(2)}, u32[]{:S(2)}) collective-permute-start(bf16[128,768]{0,1:T(8,128)(2,1)S(1)} %get-tuple-element.87), channel_id=1, source_target_pairs={{0,2},{1,3},{2,0},{3,1},{4,6},{5,7},{6,4},{7,5},{8,10},{9,11},{10,... | collective-permute-start | bytes 589832 | tf_op jit(solution)/shard_map/ppermute | solution.py:34
  207.2 37.0 %collective-permute-start.12 = (bf16[128,768]{0,1:T(8,128)(2,1)S(1)}, bf16[128,768]{0,1:T(8,128)(2,1)}, u32[]{:S(2)}, u32[]{:S(2)}) collective-permute-start(bf16[128,768]{0,1:T(8,128)(2,1)S(1)} %get-tuple-element.87), channel_id=1, source_target_pairs={{0,4},{1,5},{2,6},{3,7},{4,0},{5,1},{6,2},{7,3},{8,12},{9,13},{10,... | collective-permute-start | bytes 589832 | tf_op jit(solution)/shard_map/ppermute | solution.py:34
  213.6 30.6 %collective-permute-start.13 = (bf16[128,768]{0,1:T(8,128)(2,1)S(1)}, bf16[128,768]{0,1:T(8,128)(2,1)}, u32[]{:S(2)}, u32[]{:S(2)}) collective-permute-start(bf16[128,768]{0,1:T(8,128)(2,1)S(1)} %get-tuple-element.87), channel_id=1, source_target_pairs={{0,6},{1,7},{2,4},{3,5},{4,2},{5,3},{6,0},{7,1},{8,14},{9,15},{10,... | collective-permute-start | bytes 589832 | tf_op jit(solution)/shard_map/ppermute | solution.py:34
  221.0 31.6 %collective-permute-start.35 = (bf16[128,768]{0,1:T(8,128)(2,1)S(1)}, bf16[128,768]{0,1:T(8,128)(2,1)S(1)}, u32[]{:S(2)}, u32[]{:S(2)}) collective-permute-start(bf16[128,768]{0,1:T(8,128)(2,1)S(1)} %get-tuple-element.84), channel_id=1, source_target_pairs={{0,2},{1,3},{2,0},{3,1},{4,6},{5,7},{6,4},{7,5},{8,10},{9,11},{10,... | collective-permute-start | bytes 589832 | tf_op jit(solution)/shard_map/ppermute | solution.py:34
  221.1 39.8 %collective-permute-start.36 = (bf16[128,768]{0,1:T(8,128)(2,1)S(1)}, bf16[128,768]{0,1:T(8,128)(2,1)S(1)}, u32[]{:S(2)}, u32[]{:S(2)}) collective-permute-start(bf16[128,768]{0,1:T(8,128)(2,1)S(1)} %get-tuple-element.84), channel_id=1, source_target_pairs={{0,4},{1,5},{2,6},{3,7},{4,0},{5,1},{6,2},{7,3},{8,12},{9,13},{10,... | collective-permute-start | bytes 589832 | tf_op jit(solution)/shard_map/ppermute | solution.py:34
  233.8 28.1 %collective-permute-start.37 = (bf16[128,768]{0,1:T(8,128)(2,1)S(1)}, bf16[128,768]{0,1:T(8,128)(2,1)S(1)}, u32[]{:S(2)}, u32[]{:S(2)}) collective-permute-start(bf16[128,768]{0,1:T(8,128)(2,1)S(1)} %get-tuple-element.84), channel_id=1, source_target_pairs={{0,6},{1,7},{2,4},{3,5},{4,2},{5,3},{6,0},{7,1},{8,14},{9,15},{10,... | collective-permute-start | bytes 589832 | tf_op jit(solution)/shard_map/ppermute | solution.py:34
  244.2 23.8 %collective-permute-start.27 = (bf16[128,768]{0,1:T(8,128)(2,1)S(1)}, bf16[128,768]{0,1:T(8,128)(2,1)S(1)}, u32[]{:S(2)}, u32[]{:S(2)}) collective-permute-start(bf16[128,768]{0,1:T(8,128)(2,1)S(1)} %get-tuple-element.86), channel_id=1, source_target_pairs={{0,2},{1,3},{2,0},{3,1},{4,6},{5,7},{6,4},{7,5},{8,10},{9,11},{10,... | collective-permute-start | bytes 589832 | tf_op jit(solution)/shard_map/ppermute | solution.py:34
  244.2 25.3 %collective-permute-start.28 = (bf16[128,768]{0,1:T(8,128)(2,1)S(1)}, bf16[128,768]{0,1:T(8,128)(2,1)}, u32[]{:S(2)}, u32[]{:S(2)}) collective-permute-start(bf16[128,768]{0,1:T(8,128)(2,1)S(1)} %get-tuple-element.86), channel_id=1, source_target_pairs={{0,4},{1,5},{2,6},{3,7},{4,0},{5,1},{6,2},{7,3},{8,12},{9,13},{10,... | collective-permute-start | bytes 589832 | tf_op jit(solution)/shard_map/ppermute | solution.py:34
  262.6 35.8 %collective-permute-start.14 = (bf16[4,128,768]{1,2,0:T(8,128)(2,1)}, bf16[4,128,768]{1,2,0:T(8,128)(2,1)}, u32[]{:S(2)}, u32[]{:S(2)}) collective-permute-start(bf16[4,128,768]{1,2,0:T(8,128)(2,1)} %get-tuple-element.63), channel_id=1, source_target_pairs={{0,1},{1,0},{2,3},{3,2},{4,5},{5,4},{6,7},{7,6},{8,9},{9,8},{10,11... | collective-permute-start | bytes 2359304 | tf_op jit(solution)/shard_map/ppermute | solution.py:34
  268.0 69.9 %collective-permute-start.38 = (bf16[4,128,768]{1,2,0:T(8,128)(2,1)}, bf16[4,128,768]{1,2,0:T(8,128)(2,1)}, u32[]{:S(2)}, u32[]{:S(2)}) collective-permute-start(bf16[4,128,768]{1,2,0:T(8,128)(2,1)} %get-tuple-element.59), channel_id=1, source_target_pairs={{0,1},{1,0},{2,3},{3,2},{4,5},{5,4},{6,7},{7,6},{8,9},{9,8},{10,11... | collective-permute-start | bytes 2359304 | tf_op jit(solution)/shard_map/ppermute | solution.py:34
  271.7 48.6 %collective-permute-start.30 = (bf16[4,128,768]{1,2,0:T(8,128)(2,1)}, bf16[4,128,768]{1,2,0:T(8,128)(2,1)}, u32[]{:S(2)}, u32[]{:S(2)}) collective-permute-start(bf16[4,128,768]{1,2,0:T(8,128)(2,1)} %get-tuple-element.65), channel_id=1, source_target_pairs={{0,1},{1,0},{2,3},{3,2},{4,5},{5,4},{6,7},{7,6},{8,9},{9,8},{10,11... | collective-permute-start | bytes 2359304 | tf_op jit(solution)/shard_map/ppermute | solution.py:34
  350.5 21.2 %collective-permute-start.40 = (bf16[128,768]{1,0:T(8,128)(2,1)}, bf16[128,768]{1,0:T(8,128)(2,1)}, u32[]{:S(2)}, u32[]{:S(2)}) collective-permute-start(bf16[128,768]{1,0:T(8,128)(2,1)} %get-tuple-element.31), channel_id=1, source_target_pairs={{0,2},{1,3},{2,0},{3,1},{4,6},{5,7},{6,4},{7,5},{8,10},{9,11},{10,... | collective-permute-start | bytes 589832 | tf_op jit(solution)/shard_map/ppermute | solution.py:34
  367.8 22.4 %collective-permute-start.43 = (bf16[128,768]{1,0:T(8,128)(2,1)}, bf16[128,768]{1,0:T(8,128)(2,1)S(1)}, u32[]{:S(2)}, u32[]{:S(2)}) collective-permute-start(bf16[128,768]{1,0:T(8,128)(2,1)} %get-tuple-element.28), channel_id=1, source_target_pairs={{0,5},{1,4},{2,7},{3,6},{4,1},{5,0},{6,3},{7,2},{8,13},{9,12},{10,... | collective-permute-start | bytes 589832 | tf_op jit(solution)/shard_map/ppermute | solution.py:34
  (55 other events, 657.1 us)
Sparse Core Ops, SparseCore 0:
  215.7 31.7 all-reduce.1

commit v2 on v0

v2 whole, which is shorter than its diff:
```python
import functools

import jax
import jax.numpy as jnp
from jax import lax
from jax.experimental import pallas as pl
from jax.experimental.pallas import tpu as pltpu
from jax.sharding import PartitionSpec as P

EPSILON = 1e-06
OUTER_RATE = 0.7
OUTER_MOMENTUM = 0.9
CHUNKS = 4
TILE = 256
MESH = pl.DeviceIdType.MESH
EXACT = lax.Precision.HIGHEST
f32 = jnp.float32
bf16 = jnp.bfloat16


def partner(index, offset):
    bit = 1
    moved = index
    while bit <= offset:
        if offset & bit:
            moved = moved + bit * (1 - 2 * ((index // bit) % 2))
        bit *= 2
    return moved


def kernel(
    n,
    replicas,
    x_ref,
    frames_ref,
    mod_ref,
    gain_ref,
    w_hbm,
    cot_hbm,
    pseudo_ref,
    params_ref,
    momentum_ref,
    grad_ref,
    dw_hbm,
    table_ref,
    fragment_out,
    momentum_out,
    w_vmem,
    cot_vmem,
    sides,
    x_all,
    ni,
    ni_t,
    p_send,
    p_keep,
    p_pair,
    p_line,
    p_own,
    gathered,
    dw_vmem,
    dx_sum,
    dx_recv,
    outer_send,
    outer_recv,
    local_sem,
    dw_sem,
    outer_sem,
    x_sem,
    side_sem,
    pair_sem,
    line_sem,
    gather_line_sem,
    gather_pair_sem,
    dx_sem,
):
    dx_send = ni
    me = lax.axis_index("fsdp")
    rep = lax.axis_index("rep")
    half = n // 2
    rows = x_ref.shape[0]
    part = x_ref.shape[1] // n
    chunk = w_vmem.shape[1] // CHUNKS
    head = gain_ref.shape[1]
    frame_count = mod_ref.shape[0]
    at = [partner(me, k) for k in range(n)]
    slot = [(k % 2) * half + k // 2 for k in range(n)]

    def send(src, dst, sems, where, k):
        return pltpu.make_async_remote_copy(
            src_ref=src,
            dst_ref=dst,
            send_sem=sems.at[(0, *where)],
            recv_sem=sems.at[(1, *where)],
            device_id={"fsdp": at[k]},
            device_id_type=MESH,
        )

    def columns(k):
        return pl.ds(pl.multiple_of(at[k] * part, 128), part)

    load_w = pltpu.make_async_copy(w_hbm, w_vmem, local_sem.at[0])
    load_cot = pltpu.make_async_copy(cot_hbm, cot_vmem, local_sem.at[1])
    load_w.start()
    load_cot.start()
    outer_send[...] = pseudo_ref[...].astype(bf16)

    barrier = pltpu.get_barrier_semaphore()
    for k in range(1, n):
        pl.semaphore_signal(barrier, inc=1, device_id={"fsdp": at[k]}, device_id_type=MESH)
    for k in range(1, replicas):
        pl.semaphore_signal(
            barrier, inc=1, device_id={"rep": partner(rep, k)}, device_id_type=MESH
        )
    pl.semaphore_wait(barrier, n + replicas - 2)

    order = sorted(range(1, n), key=lambda k: -k)
    x_copies = {}
    for k in order:
        x_copies[k] = send(x_ref.at[:, columns(k)], x_all.at[slot[k]], x_sem, (k,), k)
        x_copies[k].start()

    x_f = x_ref[...].astype(f32)
    inverse = lax.rsqrt(jnp.mean(x_f * x_f, axis=-1, keepdims=True) + EPSILON)
    lane = lax.broadcasted_iota(jnp.int32, (rows, rows), 1)
    row = lax.broadcasted_iota(jnp.int32, (rows, rows), 0)
    eye = (lane == row).astype(f32)
    contract_last = (((1,), (1,)), ((), ()))
    inverse_row = jnp.sum(eye * inverse, axis=0, keepdims=True)
    side_row = lax.broadcasted_iota(jnp.int32, (8, rows), 0)
    sides[0] = jnp.where(side_row == 0, inverse_row, frames_ref[...].astype(f32))
    side_copies = {}
    for k in order:
        side_copies[k] = send(sides.at[0], sides.at[slot[k]], side_sem, (k,), k)
        side_copies[k].start()

    outer_copies = []
    for k in range(1, replicas):
        copy = pltpu.make_async_remote_copy(
            src_ref=outer_send,
            dst_ref=outer_recv.at[k - 1],
            send_sem=outer_sem.at[0, k - 1],
            recv_sem=outer_sem.at[1, k - 1],
            device_id={"rep": partner(rep, k)},
            device_id_type=MESH,
        )
        copy.start()
        outer_copies.append(copy)

    def as_columns(s):
        return lax.dot_general(
            eye, sides[s], contract_last, precision=EXACT, preferred_element_type=f32
        )

    frame_lane = lax.broadcasted_iota(jnp.int32, (rows, frame_count), 1).astype(f32)

    def modulated(cols, block):
        one_hot = (cols[:, 1:2] == frame_lane).astype(f32)
        return 1.0 + jnp.dot(one_hot, block, precision=EXACT, preferred_element_type=f32)

    own_columns = as_columns(0)
    own_mod = mod_ref[:, columns(0)]
    x_all[0] = x_ref[:, columns(0)]
    for k in [0] + order[::-1]:
        s = slot[k]
        if k:
            x_copies[k].wait_recv()
            side_copies[k].wait_recv()
        cols = as_columns(s)
        value = x_all[s].astype(f32) * cols[:, 0:1] * modulated(cols, own_mod)
        ni[s] = value.astype(bf16)
        ni_t[:, s * rows : (s + 1) * rows] = value.T.astype(bf16)
    load_w.wait()
    load_cot.wait()

    def tiles(total, body):
        size = TILE if total % TILE == 0 else TILE // 2
        lax.fori_loop(0, total // size, lambda j, carry: (body(j, size), carry)[1], 0)

    pair_copies = []
    for c in range(CHUNKS):
        for kx, target in ((1, p_send), (0, p_keep)):
            left = ni[kx * half : (kx + 1) * half].reshape(half * rows, part)

            def project(j, size, c=c, left=left, target=target):
                w = w_vmem[:, pl.ds(pl.multiple_of(c * chunk + j * size, size), size)]
                value = jnp.dot(left, w, preferred_element_type=f32).astype(bf16)
                target[c, :, :, pl.ds(pl.multiple_of(j * size, size), size)] = value.reshape(
                    half, rows, size
                )

            tiles(chunk, project)
            if kx == 1:
                copy = send(p_send.at[c], p_pair.at[c], pair_sem, (c,), 1)
                copy.start()
                pair_copies.append(copy)

    line_copies, gather_line, gather_pair = {}, {}, {}

    def reduce_pair(c):
        pair_copies[c].wait_recv()
        for kz in list(range(1, half))[::-1]:
            p_keep[c, kz] = (p_keep[c, kz].astype(f32) + p_pair[c, kz].astype(f32)).astype(bf16)
            line_copies[c, kz] = send(
                p_keep.at[c, kz], p_line.at[c, kz - 1], line_sem, (c, kz), 2 * kz
            )
            line_copies[c, kz].start()
        p_own[c % 2] = p_keep[c, 0].astype(f32) + p_pair[c, 0].astype(f32)

    def head_grads(c):
        for kz in range(1, half):
            line_copies[c, kz].wait_recv()
        gain = gain_ref[...]
        for h in range(chunk // head):
            span = slice(h * head, (h + 1) * head)
            projected = p_own[c % 2, :, span]
            for kz in range(1, half):
                projected = projected + p_line[c, kz - 1, :, span].astype(f32)
            head_inv = lax.rsqrt(
                jnp.mean(projected * projected, axis=-1, keepdims=True) + EPSILON
            )
            head_hat = projected * head_inv
            scaled = cot_vmem[:, c * chunk + h * head : c * chunk + (h + 1) * head].astype(f32) * gain
            mean = jnp.mean(scaled * head_hat, axis=-1, keepdims=True)
            gathered[c, 0, 0, :, span] = (head_inv * (scaled - head_hat * mean)).astype(bf16)
        for kz in list(range(1, half))[::-1]:
            gather_line[c, kz] = send(
                gathered.at[c, 0, 0], gathered.at[c, 0, kz], gather_line_sem, (c, kz), 2 * kz
            )
            gather_line[c, kz].start()
        gather_pair[c, 0] = send(
            gathered.at[c, 0, 0], gathered.at[c, 1, 0], gather_pair_sem, (c, 0), 1
        )
        gather_pair[c, 0].start()

    def forward(c):
        for kz in range(1, half):
            gather_line[c, kz].wait_recv()
            gather_pair[c, kz] = send(
                gathered.at[c, 0, kz], gathered.at[c, 1, kz], gather_pair_sem, (c, kz), 1
            )
            gather_pair[c, kz].start()

    def feature(c):
        for kz in range(half):
            gather_pair[c, kz].wait_recv()
        g = gathered[c].reshape(n * rows, chunk)

        def body(j, size):
            span = pl.ds(pl.multiple_of(j * size, size), size)
            w = w_vmem[span, c * chunk : (c + 1) * chunk]
            value = lax.dot_general(g, w, contract_last, preferred_element_type=f32)
            if c > 0:
                value = value + dx_sum[:, span]
            if c < CHUNKS - 1:
                dx_sum[:, span] = value
            else:
                dx_send[:, :, span] = value.astype(bf16).reshape(n, rows, size)

        tiles(part, body)

    dw_copies = []

    def weight(c):
        if c >= 2:
            dw_copies[c - 2].wait()
        g = gathered[c].reshape(n * rows, chunk)

        def body(j, size):
            span = pl.ds(pl.multiple_of(j * size, size), size)
            dw_vmem[c % 2, span, :] = jnp.dot(
                ni_t[span, :], g, preferred_element_type=f32
            ).astype(bf16)

        tiles(part, body)
        span = slice(c * chunk, (c + 1) * chunk)
        copy = pltpu.make_async_copy(dw_vmem.at[c % 2], dw_hbm.at[:, span], dw_sem.at[c])
        copy.start()
        dw_copies.append(copy)

    for t in range(CHUNKS + 3):
        if t < CHUNKS:
            reduce_pair(t)
        if 0 <= t - 1 < CHUNKS:
            head_grads(t - 1)
        if 0 <= t - 2 < CHUNKS:
            forward(t - 2)
        if 0 <= t - 3 < CHUNKS:
            feature(t - 3)
            if t - 3 < CHUNKS - 1:
                weight(t - 3)

    dx_copies = {}
    for k in order:
        dx_copies[k] = send(dx_send.at[slot[k]], dx_recv.at[slot[k]], dx_sem, (k,), k)
        dx_copies[k].start()
    weight(CHUNKS - 1)

    frame_row = lax.broadcasted_iota(jnp.int32, (frame_count, rows), 0).astype(f32)
    table = jnp.zeros((frame_count, part), f32)
    for s in range(n):
        normed = x_all[s].astype(f32) * as_columns(s)[:, 0:1]
        picked = (sides[s, 1:2, :] == frame_row).astype(f32)
        table = table + jnp.dot(
            picked, dx_send[s].astype(f32) * normed, precision=EXACT, preferred_element_type=f32
        )
    table_ref[...] = table

    for copy in outer_copies:
        copy.wait_recv()
    terms = [outer_send[...].astype(f32)] + [
        outer_recv[k - 1].astype(f32) for k in range(1, replicas)
    ]
    while len(terms) > 1:
        terms = [terms[i] + terms[i + 1] for i in range(0, len(terms), 2)]
    average = terms[0] / replicas
    new_momentum = OUTER_MOMENTUM * momentum_ref[...] + average
    momentum_out[...] = new_momentum
    fragment_out[...] = params_ref[...] - OUTER_RATE * (average + OUTER_MOMENTUM * new_momentum)

    inv = own_columns[:, 0:1]
    total = jnp.zeros((rows, 1), f32)
    for k in [0] + order[::-1]:
        s = slot[k]
        if k:
            dx_copies[k].wait_recv()
        arrived = (dx_recv if k else dx_send)[s].astype(f32)
        grad_hat = arrived * modulated(own_columns, mod_ref[:, columns(k)])
        normed = x_ref[:, columns(k)].astype(f32) * inv
        total = total + jnp.sum(grad_hat * normed, axis=-1, keepdims=True)
        dx_sum[s * rows : (s + 1) * rows, :] = grad_hat
    mean = total / (n * part)
    for k in range(n):
        s = slot[k]
        normed = x_ref[:, columns(k)].astype(f32) * inv
        grad_ref[:, columns(k)] = (
            inv * (dx_sum[s * rows : (s + 1) * rows, :] - normed * mean)
        ).astype(bf16)

    for copies in (x_copies, side_copies, line_copies, gather_line, gather_pair, dx_copies):
        for copy in copies.values():
            copy.wait_send()
    for copy in pair_copies + outer_copies:
        copy.wait_send()
    for copy in dw_copies[-2:]:
        copy.wait()


def shards(
    clip_tokens,
    frame_ids,
    modulation,
    query_gain,
    query_weight,
    query_cotangent,
    pseudo_grad,
    outer_params,
    outer_momentum,
):
    n = lax.axis_size("fsdp")
    replicas = lax.axis_size("rep")
    rows, width = clip_tokens.shape
    part = width // n
    columns = query_weight.shape[2]
    chunk = columns // CHUNKS
    half = n // 2
    head = query_gain.shape[0]
    entries = outer_params.shape[0]
    fold = (entries // 128, 128)
    vmem = pl.BlockSpec(memory_space=pltpu.VMEM)
    hbm = pl.BlockSpec(memory_space=pl.ANY)
    dma = pltpu.SemaphoreType.DMA
    shape = jax.ShapeDtypeStruct
    outs = pl.pallas_call(
        functools.partial(kernel, n, replicas),
        out_shape=(
            shape((rows, width), bf16),
            shape((part, columns), bf16),
            shape((modulation.shape[0], part), f32),
            shape(fold, f32),
            shape(fold, f32),
        ),
        in_specs=[vmem] * 4 + [hbm] * 2 + [vmem] * 3,
        out_specs=(vmem, hbm, vmem, vmem, vmem),
        scratch_shapes=[
            pltpu.VMEM((part, columns), bf16),
            pltpu.VMEM((rows, columns), bf16),
            pltpu.VMEM((n, 8, rows), f32),
            pltpu.VMEM((n, rows, part), bf16),
            pltpu.VMEM((n, rows, part), bf16),
            pltpu.VMEM((part, n * rows), bf16),
            pltpu.VMEM((CHUNKS, half, rows, chunk), bf16),
            pltpu.VMEM((CHUNKS, half, rows, chunk), bf16),
            pltpu.VMEM((CHUNKS, half, rows, chunk), bf16),
            pltpu.VMEM((CHUNKS, half - 1, rows, chunk), bf16),
            pltpu.VMEM((2, rows, chunk), f32),
            pltpu.VMEM((CHUNKS, 2, half, rows, chunk), bf16),
            pltpu.VMEM((2, part, chunk), bf16),
            pltpu.VMEM((n * rows, part), f32),
            pltpu.VMEM((n, rows, part), bf16),
            pltpu.VMEM(fold, bf16),
            pltpu.VMEM((replicas - 1, *fold), bf16),
            dma((2,)),
            dma((CHUNKS,)),
            dma((2, replicas - 1)),
            dma((2, n)),
            dma((2, n)),
            dma((2, CHUNKS)),
            dma((2, CHUNKS, half)),
            dma((2, CHUNKS, half)),
            dma((2, CHUNKS, half)),
            dma((2, n)),
        ],
        compiler_params=pltpu.CompilerParams(
            collective_id=0, has_side_effects=True, vmem_limit_bytes=60 * 2**20
        ),
    )(
        clip_tokens,
        frame_ids.reshape(1, rows),
        modulation,
        query_gain.reshape(1, head),
        query_weight[0],
        query_cotangent,
        pseudo_grad.reshape(fold),
        outer_params.reshape(fold),
        outer_momentum.reshape(fold),
    )
    input_grad, weight_grad, table_grad, new_fragment, new_momentum = outs
    return (
        input_grad,
        weight_grad[None],
        table_grad[None],
        new_fragment.reshape(entries),
        new_momentum.reshape(entries),
    )


def solution(mesh):
    placed = (
        P(("rep", "fsdp"), None),
        P(("rep", "fsdp")),
        P(),
        P(),
        P("rep", "fsdp", None),
        P(("rep", "fsdp"), None),
        P("rep", "fsdp"),
        P("fsdp"),
        P("fsdp"),
    )
    return jax.shard_map(
        shards,
        mesh=mesh,
        in_specs=placed,
        out_specs=(
            P(("rep", "fsdp"), None),
            P("rep", "fsdp", None),
            P("rep", None, "fsdp"),
            P("fsdp"),
            P("fsdp"),
        ),
        check_vma=False,
    )
```

time: 414 us -> 265 us (0.64)
  the two profiles are of different devices: /device:TPU:0 before, /device:TPU:20 now
where the time goes in v2:
time: 265 us
  Pallas kernels  255 us (96%)
  local copies, waits for them, and re-layouts  9.66 us (4%)
    pallas_call x1, Pallas kernels, shards(): pl.pallas_call(functools.partial(kernel, n, replicas), out_shape=(shape((...  255 us
    unnamed x11, local copies, waits for them, and re-layouts  9.66 us

profile of v2, /device:TPU:20, one launch (start us, length us, event | category | flops | bytes accessed | tf_op | source)
XLA Modules:
  0.0 265.1 jit_solution(10907730801974358015)
XLA Ops:
  0.6 254.8 %shard_map.128 = (bf16[128,6144]{1,0:T(8,128)(2,1)}, bf16[768,3072]{1,0:T(8,128)(2,1)}, f32[16,768]{1,0:T(8,128)}, f32[512,128]{1,0:T(8,128)}, f32[512,128]{1,0:T(8,128)}) custom-call(bf16[128,6144]{1,0:T(8,128)(2,1)} %x_ref.1, s32[1,128]{1,0:T(1,128)} %bitcast.18, f32[16,6144]{1,0:T(8,128)} %mod_ref.1, f32[1,128]{1,0:T(1,128)} %bitcast.19, ...), custom_call_target="tpu_custom_call" | custom-call | tf_op jit(solution)/shard_map/pallas_call | solution.py:373
  255.5 2.7 %copy.19 = bf16[128,6144]{1,0:T(8,128)(2,1)} copy(bf16[128,6144]{1,0:T(8,128)(2,1)} %get-tuple-element.20) | data formatting | bytes 3145728
  258.2 0.0 copy-start.2
  258.2 0.0 copy-start.1
  258.2 0.0 copy-start
  258.2 4.9 %copy.20 = bf16[1,768,3072]{2,1,0:T(8,128)(2,1)} copy(bf16[1,768,3072]{2,1,0:T(8,128)(2,1)} %bitcast.11) | data formatting | bytes 9437184
  263.1 0.0 copy-done.2
  263.1 0.6 copy.21
  263.7 0.0 copy-done.1
  263.7 0.7 copy.22
  264.4 0.0 copy-done
  264.4 0.7 copy.23
Async XLA Ops:
  258.2 4.9 %copy-start.2 = (f32[16,768]{1,0:T(8,128)S(1)}, f32[16,768]{1,0:T(8,128)}, u32[]{:S(2)}) copy-start(f32[16,768]{1,0:T(8,128)} %get-tuple-element.12) | copy-start | bytes 147460
  258.2 5.5 %copy-start.1 = (f32[512,128]{1,0:T(8,128)S(1)}, f32[512,128]{1,0:T(8,128)}, u32[]{:S(2)}) copy-start(f32[512,128]{1,0:T(8,128)} %get-tuple-element.13) | copy-start | bytes 786436
  258.2 6.3 %copy-start = (f32[512,128]{1,0:T(8,128)S(1)}, f32[512,128]{1,0:T(8,128)}, u32[]{:S(2)}) copy-start(f32[512,128]{1,0:T(8,128)} %get-tuple-element.14) | copy-start | bytes 786436

commit v3 on v2

--- a/solution.py
+++ b/solution.py
@@ -48,6 +48,7 @@
     w_vmem,
     cot_vmem,
     sides,
+    side_cols,
     x_all,
     ni,
     ni_t,
@@ -58,7 +59,7 @@
     p_own,
     gathered,
     dw_vmem,
-    dx_sum,
+    scales,
     dx_recv,
     outer_send,
     outer_recv,
@@ -114,10 +115,19 @@
     pl.semaphore_wait(barrier, n + replicas - 2)
 
     order = sorted(range(1, n), key=lambda k: -k)
-    x_copies = {}
-    for k in order:
-        x_copies[k] = send(x_ref.at[:, columns(k)], x_all.at[slot[k]], x_sem, (k,), k)
-        x_copies[k].start()
+    part_rows = rows // CHUNKS
+    spans = [pl.ds(c * part_rows, part_rows) for c in range(CHUNKS)]
+    x_copies, dx_copies = {}, {}
+
+    def send_tokens(c):
+        for k in order:
+            x_copies[c, k] = send(
+                x_ref.at[spans[c], columns(k)], x_all.at[slot[k], spans[c]], x_sem, (c, k), k
+            )
+            x_copies[c, k].start()
+
+    send_tokens(0)
+    send_tokens(1)
 
     x_f = x_ref[...].astype(f32)
     inverse = lax.rsqrt(jnp.mean(x_f * x_f, axis=-1, keepdims=True) + EPSILON)
@@ -146,29 +156,23 @@
         copy.start()
         outer_copies.append(copy)
 
-    def as_columns(s):
-        return lax.dot_general(
+    def set_columns(s):
+        side_cols[s] = lax.dot_general(
             eye, sides[s], contract_last, precision=EXACT, preferred_element_type=f32
         )
 
-    frame_lane = lax.broadcasted_iota(jnp.int32, (rows, frame_count), 1).astype(f32)
-
-    def modulated(cols, block):
-        one_hot = (cols[:, 1:2] == frame_lane).astype(f32)
+    def modulated(frames, block):
+        lanes = lax.broadcasted_iota(jnp.int32, (frames.shape[0], frame_count), 1).astype(f32)
+        one_hot = (frames == lanes).astype(f32)
         return 1.0 + jnp.dot(one_hot, block, precision=EXACT, preferred_element_type=f32)
 
-    own_columns = as_columns(0)
-    own_mod = mod_ref[:, columns(0)]
+    set_columns(0)
+    for k in range(n):
+        scales[slot[k]] = modulated(side_cols[0, :, 1:2], mod_ref[:, columns(k)])
     x_all[0] = x_ref[:, columns(0)]
-    for k in [0] + order[::-1]:
-        s = slot[k]
-        if k:
-            x_copies[k].wait_recv()
-            side_copies[k].wait_recv()
-        cols = as_columns(s)
-        value = x_all[s].astype(f32) * cols[:, 0:1] * modulated(cols, own_mod)
-        ni[s] = value.astype(bf16)
-        ni_t[:, s * rows : (s + 1) * rows] = value.T.astype(bf16)
+    for k in order[::-1]:
+        side_copies[k].wait_recv()
+        set_columns(slot[k])
     load_w.wait()
     load_cot.wait()
 
@@ -177,18 +181,26 @@
         lax.fori_loop(0, total // size, lambda j, carry: (body(j, size), carry)[1], 0)
 
     pair_copies = []
-    for c in range(CHUNKS):
+
+    def project_tokens(c):
+        for k in order[::-1]:
+            x_copies[c, k].wait_recv()
+        if c + 2 < CHUNKS:
+            send_tokens(c + 2)
+        scale = modulated(
+            side_cols[:, spans[c], 1:2].reshape(n * part_rows, 1), mod_ref[:, columns(0)]
+        )
+        normed = x_all[:, spans[c], :].astype(f32) * side_cols[:, spans[c], 0:1]
+        ni[:, spans[c], :] = (normed * scale.reshape(n, part_rows, part)).astype(bf16)
         for kx, target in ((1, p_send), (0, p_keep)):
-            left = ni[kx * half : (kx + 1) * half].reshape(half * rows, part)
-
-            def project(j, size, c=c, left=left, target=target):
-                w = w_vmem[:, pl.ds(pl.multiple_of(c * chunk + j * size, size), size)]
-                value = jnp.dot(left, w, preferred_element_type=f32).astype(bf16)
-                target[c, :, :, pl.ds(pl.multiple_of(j * size, size), size)] = value.reshape(
-                    half, rows, size
-                )
-
-            tiles(chunk, project)
+
+            def project(j, size, kx=kx, target=target):
+                span = pl.ds(pl.multiple_of(j * size, size), size)
+                left = ni[kx * half : (kx + 1) * half, spans[c], :].reshape(half * part_rows, part)
+                value = jnp.dot(left, w_vmem[:, span], preferred_element_type=f32).astype(bf16)
+                target[c, :, :, span] = value.reshape(half, part_rows, size)
+
+            tiles(w_vmem.shape[1], project)
             if kx == 1:
                 copy = send(p_send.at[c], p_pair.at[c], pair_sem, (c,), 1)
                 copy.start()
@@ -210,7 +222,7 @@
         for kz in range(1, half):
             line_copies[c, kz].wait_recv()
         gain = gain_ref[...]
-        for h in range(chunk // head):
+        for h in range(w_vmem.shape[1] // head):
             span = slice(h * head, (h + 1) * head)
             projected = p_own[c % 2, :, span]
             for kz in range(1, half):
@@ -219,122 +231,136 @@
                 jnp.mean(projected * projected, axis=-1, keepdims=True) + EPSILON
             )
             head_hat = projected * head_inv
-            scaled = cot_vmem[:, c * chunk + h * head : c * chunk + (h + 1) * head].astype(f32) * gain
+            scaled = cot_vmem[spans[c], span].astype(f32) * gain
             mean = jnp.mean(scaled * head_hat, axis=-1, keepdims=True)
-            gathered[c, 0, 0, :, span] = (head_inv * (scaled - head_hat * mean)).astype(bf16)
+            gathered[0, 0, spans[c], span] = (head_inv * (scaled - head_hat * mean)).astype(bf16)
+        own = gathered.at[0, 0, spans[c]]
         for kz in list(range(1, half))[::-1]:
             gather_line[c, kz] = send(
-                gathered.at[c, 0, 0], gathered.at[c, 0, kz], gather_line_sem, (c, kz), 2 * kz
+                own, gathered.at[0, kz, spans[c]], gather_line_sem, (c, kz), 2 * kz
             )
             gather_line[c, kz].start()
-        gather_pair[c, 0] = send(
-            gathered.at[c, 0, 0], gathered.at[c, 1, 0], gather_pair_sem, (c, 0), 1
-        )
+        gather_pair[c, 0] = send(own, gathered.at[1, 0, spans[c]], gather_pair_sem, (c, 0), 1)
         gather_pair[c, 0].start()
 
     def forward(c):
         for kz in range(1, half):
             gather_line[c, kz].wait_recv()
             gather_pair[c, kz] = send(
-                gathered.at[c, 0, kz], gathered.at[c, 1, kz], gather_pair_sem, (c, kz), 1
+                gathered.at[0, kz, spans[c]],
+                gathered.at[1, kz, spans[c]],
+                gather_pair_sem,
+                (c, kz),
+                1,
             )
             gather_pair[c, kz].start()
 
     def feature(c):
         for kz in range(half):
             gather_pair[c, kz].wait_recv()
-        g = gathered[c].reshape(n * rows, chunk)
 
         def body(j, size):
             span = pl.ds(pl.multiple_of(j * size, size), size)
-            w = w_vmem[span, c * chunk : (c + 1) * chunk]
-            value = lax.dot_general(g, w, contract_last, preferred_element_type=f32)
-            if c > 0:
-                value = value + dx_sum[:, span]
-            if c < CHUNKS - 1:
-                dx_sum[:, span] = value
-            else:
-                dx_send[:, :, span] = value.astype(bf16).reshape(n, rows, size)
+            g = gathered[:, :, spans[c], :].reshape(n * part_rows, w_vmem.shape[1])
+            value = lax.dot_general(g, w_vmem[span, :], contract_last, preferred_element_type=f32)
+            dx_send[:, spans[c], span] = value.astype(bf16).reshape(n, part_rows, size)
 
         tiles(part, body)
+        for k in order:
+            dx_copies[c, k] = send(
+                dx_send.at[slot[k], spans[c]], dx_recv.at[slot[k], spans[c]], dx_sem, (c, k), k
+            )
+            dx_copies[c, k].start()
 
     dw_copies = []
 
     def weight(c):
         if c >= 2:
             dw_copies[c - 2].wait()
-        g = gathered[c].reshape(n * rows, chunk)
+        span = slice(c * chunk, (c + 1) * chunk)
 
         def body(j, size):
-            span = pl.ds(pl.multiple_of(j * size, size), size)
-            dw_vmem[c % 2, span, :] = jnp.dot(
-                ni_t[span, :], g, preferred_element_type=f32
+            lines = pl.ds(pl.multiple_of(j * size, size), size)
+            g = gathered[:, :, :, span].reshape(n * rows, chunk)
+            dw_vmem[c % 2, lines, :] = jnp.dot(
+                ni_t[lines, :], g, preferred_element_type=f32
             ).astype(bf16)
 
         tiles(part, body)
-        span = slice(c * chunk, (c + 1) * chunk)
         copy = pltpu.make_async_copy(dw_vmem.at[c % 2], dw_hbm.at[:, span], dw_sem.at[c])
         copy.start()
         dw_copies.append(copy)
 
-    for t in range(CHUNKS + 3):
+    def finish(c):
+        inv = side_cols[0, spans[c], 0:1]
+        total = jnp.zeros((part_rows, 1), f32)
+        for k in [0] + order[::-1]:
+            s = slot[k]
+            if k:
+                dx_copies[c, k].wait_recv()
+            arrived = (dx_recv if k else dx_send)[s, spans[c], :].astype(f32)
+            grad_hat = arrived * scales[s, spans[c], :]
+            normed = x_ref[spans[c], columns(k)].astype(f32) * inv
+            total = total + jnp.sum(grad_hat * normed, axis=-1, keepdims=True)
+            scales[s, spans[c], :] = grad_hat
+        mean = total / (n * part)
+        for k in range(n):
+            normed = x_ref[spans[c], columns(k)].astype(f32) * inv
+            grad_ref[spans[c], columns(k)] = (
+                inv * (scales[slot[k], spans[c], :] - normed * mean)
+            ).astype(bf16)
+
+    def outer_step():
+        for copy in outer_copies:
+            copy.wait_recv()
+        terms = [outer_send[...].astype(f32)] + [
+            outer_recv[k - 1].astype(f32) for k in range(1, replicas)
+        ]
+        while len(terms) > 1:
+            terms = [terms[i] + terms[i + 1] for i in range(0, len(terms), 2)]
+        average = terms[0] / replicas
+        new_momentum = OUTER_MOMENTUM * momentum_ref[...] + average
+        momentum_out[...] = new_momentum
+        fragment_out[...] = params_ref[...] - OUTER_RATE * (
+            average + OUTER_MOMENTUM * new_momentum
+        )
+
+    def table():
+        frame_row = lax.broadcasted_iota(jnp.int32, (frame_count, rows), 0).astype(f32)
+        summed = jnp.zeros((frame_count, part), f32)
+        for s in range(n):
+            normed = x_all[s].astype(f32) * side_cols[s, :, 0:1]
+            picked = (sides[s, 1:2, :] == frame_row).astype(f32)
+            summed = summed + jnp.dot(
+                picked,
+                dx_send[s].astype(f32) * normed,
+                precision=EXACT,
+                preferred_element_type=f32,
+            )
+        table_ref[...] = summed
+
+    for t in range(CHUNKS + 4):
         if t < CHUNKS:
-            reduce_pair(t)
+            project_tokens(t)
+        if t == CHUNKS - 1:
+            for s in range(n):
+                ni_t[:, s * rows : (s + 1) * rows] = ni[s].astype(f32).T.astype(bf16)
         if 0 <= t - 1 < CHUNKS:
-            head_grads(t - 1)
+            reduce_pair(t - 1)
+        if t == CHUNKS:
+            outer_step()
         if 0 <= t - 2 < CHUNKS:
-            forward(t - 2)
+            head_grads(t - 2)
         if 0 <= t - 3 < CHUNKS:
-            feature(t - 3)
-            if t - 3 < CHUNKS - 1:
-                weight(t - 3)
-
-    dx_copies = {}
-    for k in order:
-        dx_copies[k] = send(dx_send.at[slot[k]], dx_recv.at[slot[k]], dx_sem, (k,), k)
-        dx_copies[k].start()
-    weight(CHUNKS - 1)
-
-    frame_row = lax.broadcasted_iota(jnp.int32, (frame_count, rows), 0).astype(f32)
-    table = jnp.zeros((frame_count, part), f32)
-    for s in range(n):
-        normed = x_all[s].astype(f32) * as_columns(s)[:, 0:1]
-        picked = (sides[s, 1:2, :] == frame_row).astype(f32)
-        table = table + jnp.dot(
-            picked, dx_send[s].astype(f32) * normed, precision=EXACT, preferred_element_type=f32
-        )
-    table_ref[...] = table
-
-    for copy in outer_copies:
-        copy.wait_recv()
-    terms = [outer_send[...].astype(f32)] + [
-        outer_recv[k - 1].astype(f32) for k in range(1, replicas)
-    ]
-    while len(terms) > 1:
-        terms = [terms[i] + terms[i + 1] for i in range(0, len(terms), 2)]
-    average = terms[0] / replicas
-    new_momentum = OUTER_MOMENTUM * momentum_ref[...] + average
-    momentum_out[...] = new_momentum
-    fragment_out[...] = params_ref[...] - OUTER_RATE * (average + OUTER_MOMENTUM * new_momentum)
-
-    inv = own_columns[:, 0:1]
-    total = jnp.zeros((rows, 1), f32)
-    for k in [0] + order[::-1]:
-        s = slot[k]
-        if k:
-            dx_copies[k].wait_recv()
-        arrived = (dx_recv if k else dx_send)[s].astype(f32)
-        grad_hat = arrived * modulated(own_columns, mod_ref[:, columns(k)])
-        normed = x_ref[:, columns(k)].astype(f32) * inv
-        total = total + jnp.sum(grad_hat * normed, axis=-1, keepdims=True)
-        dx_sum[s * rows : (s + 1) * rows, :] = grad_hat
-    mean = total / (n * part)
-    for k in range(n):
-        s = slot[k]
-        normed = x_ref[:, columns(k)].astype(f32) * inv
-        grad_ref[:, columns(k)] = (
-            inv * (dx_sum[s * rows : (s + 1) * rows, :] - normed * mean)
-        ).astype(bf16)
+            forward(t - 3)
+        if 0 <= t - 4 < CHUNKS:
+            feature(t - 4)
+    for c in range(CHUNKS):
+        weight(c)
+        if c < CHUNKS - 1:
+            finish(c)
+    table()
+    finish(CHUNKS - 1)
 
     for copies in (x_copies, side_copies, line_copies, gather_line, gather_pair, dx_copies):
         for copy in copies.values():
@@ -362,6 +388,7 @@
     part = width // n
     columns = query_weight.shape[2]
     chunk = columns // CHUNKS
+    part_rows = rows // CHUNKS
     half = n // 2
     head = query_gain.shape[0]
     entries = outer_params.shape[0]
@@ -385,33 +412,34 @@
             pltpu.VMEM((part, columns), bf16),
             pltpu.VMEM((rows, columns), bf16),
             pltpu.VMEM((n, 8, rows), f32),
+            pltpu.VMEM((n, rows, 8), f32),
             pltpu.VMEM((n, rows, part), bf16),
             pltpu.VMEM((n, rows, part), bf16),
             pltpu.VMEM((part, n * rows), bf16),
-            pltpu.VMEM((CHUNKS, half, rows, chunk), bf16),
-            pltpu.VMEM((CHUNKS, half, rows, chunk), bf16),
-            pltpu.VMEM((CHUNKS, half, rows, chunk), bf16),
-            pltpu.VMEM((CHUNKS, half - 1, rows, chunk), bf16),
-            pltpu.VMEM((2, rows, chunk), f32),
-            pltpu.VMEM((CHUNKS, 2, half, rows, chunk), bf16),
+            pltpu.VMEM((CHUNKS, half, part_rows, columns), bf16),
+            pltpu.VMEM((CHUNKS, half, part_rows, columns), bf16),
+            pltpu.VMEM((CHUNKS, half, part_rows, columns), bf16),
+            pltpu.VMEM((CHUNKS, half - 1, part_rows, columns), bf16),
+            pltpu.VMEM((2, part_rows, columns), f32),
+            pltpu.VMEM((2, half, rows, columns), bf16),
             pltpu.VMEM((2, part, chunk), bf16),
-            pltpu.VMEM((n * rows, part), f32),
+            pltpu.VMEM((n, rows, part), f32),
             pltpu.VMEM((n, rows, part), bf16),
             pltpu.VMEM(fold, bf16),
             pltpu.VMEM((replicas - 1, *fold), bf16),
             dma((2,)),
             dma((CHUNKS,)),
             dma((2, replicas - 1)),
-            dma((2, n)),
+            dma((2, CHUNKS, n)),
             dma((2, n)),
             dma((2, CHUNKS)),
             dma((2, CHUNKS, half)),
             dma((2, CHUNKS, half)),
             dma((2, CHUNKS, half)),
-            dma((2, n)),
+            dma((2, CHUNKS, n)),
         ],
         compiler_params=pltpu.CompilerParams(
-            collective_id=0, has_side_effects=True, vmem_limit_bytes=60 * 2**20
+            collective_id=0, has_side_effects=True, vmem_limit_bytes=62 * 2**20
         ),
     )(
         clip_tokens,

time: 265 us -> 247 us (0.932)
  the two profiles are of different devices: /device:TPU:20 before, /device:TPU:0 now
where the time goes in v3:
time: 247 us
  Pallas kernels  237 us (96%)
  local copies, waits for them, and re-layouts  9.66 us (4%)
    pallas_call x1, Pallas kernels, shards(): pl.pallas_call(functools.partial(kernel, n, replicas), out_shape=(shape((...  237 us
    unnamed x11, local copies, waits for them, and re-layouts  9.66 us

profile of v3, /device:TPU:0, one launch (start us, length us, event | category | flops | bytes accessed | tf_op | source)
XLA Modules:
  0.0 246.9 jit_solution(15027842219767369399)
XLA Ops:
  0.6 236.6 %shard_map.128 = (bf16[128,6144]{1,0:T(8,128)(2,1)}, bf16[768,3072]{1,0:T(8,128)(2,1)}, f32[16,768]{1,0:T(8,128)}, f32[512,128]{1,0:T(8,128)}, f32[512,128]{1,0:T(8,128)}) custom-call(bf16[128,6144]{1,0:T(8,128)(2,1)} %x_ref.1, s32[1,128]{1,0:T(1,128)} %bitcast.18, f32[16,6144]{1,0:T(8,128)} %mod_ref.1, f32[1,128]{1,0:T(1,128)} %bitcast.19, ...), custom_call_target="tpu_custom_call" | custom-call | tf_op jit(solution)/shard_map/pallas_call | solution.py:400
  237.2 2.7 %copy.19 = bf16[128,6144]{1,0:T(8,128)(2,1)} copy(bf16[128,6144]{1,0:T(8,128)(2,1)} %get-tuple-element.20) | data formatting | bytes 3145728
  239.9 0.0 copy-start.2
  239.9 0.0 copy-start.1
  239.9 0.0 copy-start
  239.9 4.9 %copy.20 = bf16[1,768,3072]{2,1,0:T(8,128)(2,1)} copy(bf16[1,768,3072]{2,1,0:T(8,128)(2,1)} %bitcast.11) | data formatting | bytes 9437184
  244.8 0.0 copy-done.2
  244.8 0.6 copy.21
  245.4 0.0 copy-done.1
  245.4 0.7 copy.22
  246.2 0.0 copy-done
  246.2 0.7 copy.23
Async XLA Ops:
  239.9 4.9 %copy-start.2 = (f32[16,768]{1,0:T(8,128)S(1)}, f32[16,768]{1,0:T(8,128)}, u32[]{:S(2)}) copy-start(f32[16,768]{1,0:T(8,128)} %get-tuple-element.12) | copy-start | bytes 147460
  239.9 5.5 %copy-start.1 = (f32[512,128]{1,0:T(8,128)S(1)}, f32[512,128]{1,0:T(8,128)}, u32[]{:S(2)}) copy-start(f32[512,128]{1,0:T(8,128)} %get-tuple-element.13) | copy-start | bytes 786436
  239.9 6.3 %copy-start = (f32[512,128]{1,0:T(8,128)S(1)}, f32[512,128]{1,0:T(8,128)}, u32[]{:S(2)}) copy-start(f32[512,128]{1,0:T(8,128)} %get-tuple-element.14) | copy-start | bytes 786436

commit v4 on v3

--- a/solution.py
+++ b/solution.py
@@ -72,6 +72,7 @@
     line_sem,
     gather_line_sem,
     gather_pair_sem,
+    pass_sem,
     dx_sem,
 ):
     dx_send = ni
@@ -180,6 +181,9 @@
         size = TILE if total % TILE == 0 else TILE // 2
         lax.fori_loop(0, total // size, lambda j, carry: (body(j, size), carry)[1], 0)
 
+    passed_on = half == 4
+    inner = (me // 2 + 1) // 2 == 1
+    passes = {}
     pair_copies = []
 
     def project_tokens(c):
@@ -236,16 +240,29 @@
             gathered[0, 0, spans[c], span] = (head_inv * (scaled - head_hat * mean)).astype(bf16)
         own = gathered.at[0, 0, spans[c]]
         for kz in list(range(1, half))[::-1]:
+            source = gathered.at[0, 1, spans[c]] if passed_on and kz == 2 else own
+            target = 3 if passed_on and kz == 2 else kz
             gather_line[c, kz] = send(
-                own, gathered.at[0, kz, spans[c]], gather_line_sem, (c, kz), 2 * kz
-            )
-            gather_line[c, kz].start()
+                source, gathered.at[0, kz, spans[c]], gather_line_sem, (c, kz), 2 * target
+            )
+            if not passed_on or kz == 1:
+                gather_line[c, kz].start()
+        if passed_on:
+            pl.when(inner)(gather_line[c, 3].start)
+            for i, kz in enumerate((3, 2)):
+                passes[c, i] = pltpu.make_async_remote_copy(
+                    src_ref=gathered.at[0, kz, spans[c]],
+                    dst_ref=gathered.at[0, 5 - kz, spans[c]],
+                    send_sem=pass_sem.at[c, i],
+                    recv_sem=gather_line_sem.at[1, c, 5 - kz],
+                    device_id={"fsdp": at[2]},
+                    device_id_type=MESH,
+                )
         gather_pair[c, 0] = send(own, gathered.at[1, 0, spans[c]], gather_pair_sem, (c, 0), 1)
         gather_pair[c, 0].start()
 
-    def forward(c):
-        for kz in range(1, half):
-            gather_line[c, kz].wait_recv()
+    def pair_forward(c, kz):
+        if (c, kz) not in gather_pair:
             gather_pair[c, kz] = send(
                 gathered.at[0, kz, spans[c]],
                 gathered.at[1, kz, spans[c]],
@@ -253,7 +270,49 @@
                 (c, kz),
                 1,
             )
-            gather_pair[c, kz].start()
+        gather_pair[c, kz].start()
+
+    def forward(c, stage):
+        if not passed_on:
+            if stage == 0:
+                for kz in range(1, half):
+                    gather_line[c, kz].wait_recv()
+                    pair_forward(c, kz)
+            return
+
+        if stage == 0:
+            gather_line[c, 1].wait_recv()
+
+            @pl.when(inner)
+            def pass_first():
+                gather_line[c, 2].start()
+
+            pair_forward(c, 1)
+            gather_pair[c, 3] = send(
+                gathered.at[0, 3, spans[c]],
+                gathered.at[1, 3, spans[c]],
+                gather_pair_sem,
+                (c, 3),
+                1,
+            )
+
+            @pl.when(inner)
+            def pass_second():
+                gather_line[c, 3].wait_recv()
+                passes[c, 0].start()
+                gather_pair[c, 3].start()
+
+        if stage == 1:
+            gather_line[c, 2].wait_recv()
+            pl.when(inner)(passes[c, 1].start)
+            pair_forward(c, 2)
+
+        if stage == 2:
+
+            @pl.when(jnp.logical_not(inner))
+            def last():
+                gather_line[c, 3].wait_recv()
+                gather_pair[c, 3].start()
 
     def feature(c):
         for kz in range(half):
@@ -345,14 +404,19 @@
         if t == CHUNKS - 1:
             for s in range(n):
                 ni_t[:, s * rows : (s + 1) * rows] = ni[s].astype(f32).T.astype(bf16)
+        ready = 0 <= t - 3 < CHUNKS
+        if ready:
+            forward(t - 3, 0)
         if 0 <= t - 1 < CHUNKS:
             reduce_pair(t - 1)
         if t == CHUNKS:
             outer_step()
+        if ready:
+            forward(t - 3, 1)
         if 0 <= t - 2 < CHUNKS:
             head_grads(t - 2)
-        if 0 <= t - 3 < CHUNKS:
-            forward(t - 3)
+        if ready:
+            forward(t - 3, 2)
         if 0 <= t - 4 < CHUNKS:
             feature(t - 4)
     for c in range(CHUNKS):
@@ -362,9 +426,20 @@
     table()
     finish(CHUNKS - 1)
 
-    for copies in (x_copies, side_copies, line_copies, gather_line, gather_pair, dx_copies):
+    for copies in (x_copies, side_copies, line_copies, gather_pair, dx_copies):
         for copy in copies.values():
             copy.wait_send()
+    for (c, kz), copy in gather_line.items():
+        if not passed_on or kz == 1:
+            copy.wait_send()
+    if passed_on:
+
+        @pl.when(inner)
+        def sent():
+            for c in range(CHUNKS):
+                for copy in (gather_line[c, 2], gather_line[c, 3], passes[c, 0], passes[c, 1]):
+                    copy.wait_send()
+
     for copy in pair_copies + outer_copies:
         copy.wait_send()
     for copy in dw_copies[-2:]:
@@ -436,6 +511,7 @@
             dma((2, CHUNKS, half)),
             dma((2, CHUNKS, half)),
             dma((2, CHUNKS, half)),
+            dma((CHUNKS, 2)),
             dma((2, CHUNKS, n)),
         ],
         compiler_params=pltpu.CompilerParams(

time: 247 us -> 226 us (0.915)
  Pallas kernels: 237 us -> 215 us
    pallas_call x1, Pallas kernels: 237 us -> 215 us  [shards(): pl.pallas_call(functools.partial(kernel, n, replicas), out_shape=(shape((...]
where the time goes in v4:
time: 226 us; the launch traced here: 225 us
  Pallas kernels  215 us (95%)
  local copies, waits for them, and re-layouts  9.66 us (4%)
    pallas_call x1, Pallas kernels, shards(): pl.pallas_call(functools.partial(kernel, n, replicas), out_shape=(shape((...  215 us
    unnamed x11, local copies, waits for them, and re-layouts  9.66 us

profile of v4, /device:TPU:0, one launch (start us, length us, event | category | flops | bytes accessed | tf_op | source)
XLA Modules:
  0.0 225.4 jit_solution(10411121068363107702)
XLA Ops:
  0.6 215.1 %shard_map.128 = (bf16[128,6144]{1,0:T(8,128)(2,1)}, bf16[768,3072]{1,0:T(8,128)(2,1)}, f32[16,768]{1,0:T(8,128)}, f32[512,128]{1,0:T(8,128)}, f32[512,128]{1,0:T(8,128)}) custom-call(bf16[128,6144]{1,0:T(8,128)(2,1)} %x_ref.1, s32[1,128]{1,0:T(1,128)} %bitcast.18, f32[16,6144]{1,0:T(8,128)} %mod_ref.1, f32[1,128]{1,0:T(1,128)} %bitcast.19, ...), custom_call_target="tpu_custom_call" | custom-call | tf_op jit(solution)/shard_map/pallas_call | solution.py:475
  215.8 2.7 %copy.19 = bf16[128,6144]{1,0:T(8,128)(2,1)} copy(bf16[128,6144]{1,0:T(8,128)(2,1)} %get-tuple-element.20) | data formatting | bytes 3145728
  218.5 0.0 copy-start.2
  218.5 0.0 copy-start.1
  218.5 0.0 copy-start
  218.5 4.9 %copy.20 = bf16[1,768,3072]{2,1,0:T(8,128)(2,1)} copy(bf16[1,768,3072]{2,1,0:T(8,128)(2,1)} %bitcast.11) | data formatting | bytes 9437184
  223.4 0.0 copy-done.2
  223.4 0.6 copy.21
  224.0 0.0 copy-done.1
  224.0 0.7 copy.22
  224.7 0.0 copy-done
  224.7 0.7 copy.23
Async XLA Ops:
  218.5 4.9 %copy-start.2 = (f32[16,768]{1,0:T(8,128)S(1)}, f32[16,768]{1,0:T(8,128)}, u32[]{:S(2)}) copy-start(f32[16,768]{1,0:T(8,128)} %get-tuple-element.12) | copy-start | bytes 147460
  218.5 5.5 %copy-start.1 = (f32[512,128]{1,0:T(8,128)S(1)}, f32[512,128]{1,0:T(8,128)}, u32[]{:S(2)}) copy-start(f32[512,128]{1,0:T(8,128)} %get-tuple-element.13) | copy-start | bytes 786436
  218.5 6.3 %copy-start = (f32[512,128]{1,0:T(8,128)S(1)}, f32[512,128]{1,0:T(8,128)}, u32[]{:S(2)}) copy-start(f32[512,128]{1,0:T(8,128)} %get-tuple-element.14) | copy-start | bytes 786436

commit v5 on v4

--- a/solution.py
+++ b/solution.py
@@ -56,6 +56,7 @@
     p_keep,
     p_pair,
     p_line,
+    cross,
     p_own,
     gathered,
     dw_vmem,
@@ -70,6 +71,7 @@
     side_sem,
     pair_sem,
     line_sem,
+    cross_sem,
     gather_line_sem,
     gather_pair_sem,
     pass_sem,
@@ -183,7 +185,7 @@
 
     passed_on = half == 4
     inner = (me // 2 + 1) // 2 == 1
-    passes = {}
+    passes, crossing = {}, {}
     pair_copies = []
 
     def project_tokens(c):
@@ -217,19 +219,64 @@
         for kz in list(range(1, half))[::-1]:
             p_keep[c, kz] = (p_keep[c, kz].astype(f32) + p_pair[c, kz].astype(f32)).astype(bf16)
             line_copies[c, kz] = send(
-                p_keep.at[c, kz], p_line.at[c, kz - 1], line_sem, (c, kz), 2 * kz
-            )
-            line_copies[c, kz].start()
+                p_keep.at[c, kz],
+                p_line.at[c, kz - 1],
+                line_sem,
+                (c, kz),
+                2 if passed_on else 2 * kz,
+            )
+            if passed_on:
+                pl.when(jnp.logical_not(inner))(line_copies[c, kz].start)
+            else:
+                line_copies[c, kz].start()
+        if passed_on:
+            for kz in (2, 3):
+                crossing[c, kz] = send(
+                    p_keep.at[c, kz], cross.at[c, kz - 2], cross_sem, (c, kz - 2), 6
+                )
         p_own[c % 2] = p_keep[c, 0].astype(f32) + p_pair[c, 0].astype(f32)
 
+    def add_keep(c, kz, other):
+        p_keep[c, kz] = (p_keep[c, kz].astype(f32) + other.astype(f32)).astype(bf16)
+
+    def reduce_line(c, stage):
+        if not passed_on:
+            return
+
+        @pl.when(inner)
+        def combine():
+            if stage == 0:
+                line_copies[c, 3].wait_recv()
+                add_keep(c, 2, p_line[c, 2])
+                crossing[c, 2].start()
+                line_copies[c, 2].wait_recv()
+                add_keep(c, 3, p_line[c, 1])
+                crossing[c, 3].start()
+                line_copies[c, 1].wait_recv()
+                p_own[c % 2] = p_own[c % 2] + p_line[c, 0].astype(f32)
+            else:
+                crossing[c, 2].wait_recv()
+                add_keep(c, 1, cross[c, 0])
+                line_copies[c, 1].start()
+                crossing[c, 3].wait_recv()
+                p_own[c % 2] = p_own[c % 2] + cross[c, 1].astype(f32)
+
+        if stage == 1:
+
+            @pl.when(jnp.logical_not(inner))
+            def arrive():
+                line_copies[c, 1].wait_recv()
+                p_own[c % 2] = p_own[c % 2] + p_line[c, 0].astype(f32)
+
     def head_grads(c):
-        for kz in range(1, half):
-            line_copies[c, kz].wait_recv()
+        if not passed_on:
+            for kz in range(1, half):
+                line_copies[c, kz].wait_recv()
         gain = gain_ref[...]
         for h in range(w_vmem.shape[1] // head):
             span = slice(h * head, (h + 1) * head)
             projected = p_own[c % 2, :, span]
-            for kz in range(1, half):
+            for kz in range(1, 1 if passed_on else half):
                 projected = projected + p_line[c, kz - 1, :, span].astype(f32)
             head_inv = lax.rsqrt(
                 jnp.mean(projected * projected, axis=-1, keepdims=True) + EPSILON
@@ -405,8 +452,13 @@
             for s in range(n):
                 ni_t[:, s * rows : (s + 1) * rows] = ni[s].astype(f32).T.astype(bf16)
         ready = 0 <= t - 3 < CHUNKS
+        reducing = 0 <= t - 2 < CHUNKS
+        if reducing:
+            reduce_line(t - 2, 0)
         if ready:
             forward(t - 3, 0)
+        if reducing:
+            reduce_line(t - 2, 1)
         if 0 <= t - 1 < CHUNKS:
             reduce_pair(t - 1)
         if t == CHUNKS:
@@ -426,8 +478,11 @@
     table()
     finish(CHUNKS - 1)
 
-    for copies in (x_copies, side_copies, line_copies, gather_pair, dx_copies):
+    for copies in (x_copies, side_copies, gather_pair, dx_copies):
         for copy in copies.values():
+            copy.wait_send()
+    for (c, kz), copy in line_copies.items():
+        if not passed_on or kz == 1:
             copy.wait_send()
     for (c, kz), copy in gather_line.items():
         if not passed_on or kz == 1:
@@ -439,6 +494,14 @@
             for c in range(CHUNKS):
                 for copy in (gather_line[c, 2], gather_line[c, 3], passes[c, 0], passes[c, 1]):
                     copy.wait_send()
+                crossing[c, 2].wait_send()
+                crossing[c, 3].wait_send()
+
+        @pl.when(jnp.logical_not(inner))
+        def sent_outer():
+            for c in range(CHUNKS):
+                line_copies[c, 2].wait_send()
+                line_copies[c, 3].wait_send()
 
     for copy in pair_copies + outer_copies:
         copy.wait_send()
@@ -495,6 +558,7 @@
             pltpu.VMEM((CHUNKS, half, part_rows, columns), bf16),
             pltpu.VMEM((CHUNKS, half, part_rows, columns), bf16),
             pltpu.VMEM((CHUNKS, half - 1, part_rows, columns), bf16),
+            pltpu.VMEM((CHUNKS, 2, part_rows, columns) if half == 4 else (1, 1, 16, 128), bf16),
             pltpu.VMEM((2, part_rows, columns), f32),
             pltpu.VMEM((2, half, rows, columns), bf16),
             pltpu.VMEM((2, part, chunk), bf16),
@@ -509,6 +573,7 @@
             dma((2, n)),
             dma((2, CHUNKS)),
             dma((2, CHUNKS, half)),
+            dma((2, CHUNKS, 2)),
             dma((2, CHUNKS, half)),
             dma((2, CHUNKS, half)),
             dma((CHUNKS, 2)),

time: 226 us -> 213 us (0.942)
  Pallas kernels: 215 us -> 203 us
    pallas_call x1, Pallas kernels: 215 us -> 203 us  [shards(): pl.pallas_call(functools.partial(kernel, n, replicas), out_shape=(shape((...]
where the time goes in v5:
time: 213 us
  Pallas kernels  203 us (95%)
  local copies, waits for them, and re-layouts  9.66 us (5%)
    pallas_call x1, Pallas kernels, shards(): pl.pallas_call(functools.partial(kernel, n, replicas), out_shape=(shape((...  203 us
    unnamed x11, local copies, waits for them, and re-layouts  9.66 us

profile of v5, /device:TPU:0, one launch (start us, length us, event | category | flops | bytes accessed | tf_op | source)
XLA Modules:
  0.0 213.1 jit_solution(6047329354151900796)
XLA Ops:
  0.6 202.8 %shard_map.128 = (bf16[128,6144]{1,0:T(8,128)(2,1)}, bf16[768,3072]{1,0:T(8,128)(2,1)}, f32[16,768]{1,0:T(8,128)}, f32[512,128]{1,0:T(8,128)}, f32[512,128]{1,0:T(8,128)}) custom-call(bf16[128,6144]{1,0:T(8,128)(2,1)} %x_ref.1, s32[1,128]{1,0:T(1,128)} %bitcast.18, f32[16,6144]{1,0:T(8,128)} %mod_ref.1, f32[1,128]{1,0:T(1,128)} %bitcast.19, ...), custom_call_target="tpu_custom_call" | custom-call | tf_op jit(solution)/shard_map/pallas_call | solution.py:538
  203.4 2.7 %copy.19 = bf16[128,6144]{1,0:T(8,128)(2,1)} copy(bf16[128,6144]{1,0:T(8,128)(2,1)} %get-tuple-element.20) | data formatting | bytes 3145728
  206.1 0.0 copy-start.2
  206.1 0.0 copy-start.1
  206.1 0.0 copy-start
  206.1 4.9 %copy.20 = bf16[1,768,3072]{2,1,0:T(8,128)(2,1)} copy(bf16[1,768,3072]{2,1,0:T(8,128)(2,1)} %bitcast.11) | data formatting | bytes 9437184
  211.0 0.0 copy-done.2
  211.0 0.6 copy.21
  211.7 0.0 copy-done.1
  211.7 0.7 copy.22
  212.4 0.0 copy-done
  212.4 0.7 copy.23
Async XLA Ops:
  206.1 4.9 %copy-start.2 = (f32[16,768]{1,0:T(8,128)S(1)}, f32[16,768]{1,0:T(8,128)}, u32[]{:S(2)}) copy-start(f32[16,768]{1,0:T(8,128)} %get-tuple-element.12) | copy-start | bytes 147460
  206.1 5.5 %copy-start.1 = (f32[512,128]{1,0:T(8,128)S(1)}, f32[512,128]{1,0:T(8,128)}, u32[]{:S(2)}) copy-start(f32[512,128]{1,0:T(8,128)} %get-tuple-element.13) | copy-start | bytes 786436
  206.1 6.3 %copy-start = (f32[512,128]{1,0:T(8,128)S(1)}, f32[512,128]{1,0:T(8,128)}, u32[]{:S(2)}) copy-start(f32[512,128]{1,0:T(8,128)} %get-tuple-element.14) | copy-start | bytes 786436
